TPU v7x, 128 devices: a whole 4x4x4 slice. The times are simulated.
128 devices in a mesh: req: 32 (over y, z, x_hi), kvh: 4 (over x_lo, core).
Axes of the slice: x: 4 (x_hi: 2, x_lo: 2; x = x_hi * 2 + x_lo), y: 4, z: 4, core: 2. Of those that a mesh axis runs over, the one named last changes fastest.
Arguments:
- queries: bfloat16 [1536, 8192], P('req', 'kvh'), may hold values from -64 to 64
- keys: bfloat16 [1536, 4, 192, 128], P('req', 'kvh'), may hold values from -4 to 4
- values: bfloat16 [1536, 4, 192, 128], P('req', 'kvh'), may hold values from -5 to 5
- lengths: int32 [1536], P('req'), may hold values from 2 to 192, as said below
- o_proj: bfloat16 [8192, 4096], P('kvh', 'req'), may hold values from -0.5 to 0.5
- residual: bfloat16 [1536, 4096], P(('req', 'kvh')), may hold values from -6 to 6
- norm_gain: float32 [4096], replicated, may hold values from 0.1 to 1.9
- gate_up: bfloat16 [128, 4096, 1536], P(('req', 'kvh')), may hold values from -0.09375 to 0.09375
- down: bfloat16 [128, 768, 4096], P(('req', 'kvh')), may hold values from -0.21875 to 0.21875
- routes: int32 [1536, 8], P(('req', 'kvh')), may hold values from 0 to 127, all different within a row; in each aligned block of 12 rows (0 to 11, 12 to 23, ...) at most 2 rows name the same one
- route_weights: float32 [1536, 8], P(('req', 'kvh')), may hold values from 0.05 to 0.5
Outputs:
- mixed: bfloat16 [1536, 4096], P(('req', 'kvh'))
Inputs may be any that keep to these rules, and one draw needn't show every extreme that they name: `lengths`: request 0 has all 192 positions. `routes`: among the 12 rows of one device, no expert is named by more than 2 rows.
All inputs are finite; a program needn't handle non-finite values.
Results may differ from a plain program's by a relative error of at most 0.0056.
Values may be sent and summed in bfloat16 or wider, within the bound.
A program may use at most 128 MiB of HBM per device.

v0:
```python
import math

import jax
import jax.numpy as jnp
from jax import lax
from jax.sharding import PartitionSpec as P


def attend(queries, keys, values, lengths):
    rows = queries.shape[0]
    width = keys.shape[3]
    group = queries.shape[1] // width
    query_heads = queries.reshape(rows, group, width)
    scores = jnp.einsum(
        "rgd,rpd->rgp", query_heads, keys[:, 0], preferred_element_type=jnp.float32
    ) / math.sqrt(width)
    valid = lax.broadcasted_iota(jnp.int32, (rows, keys.shape[2]), 1) < lengths[:, None]
    scores = jnp.where(valid[:, None, :], scores, -1e30)
    shifted = jnp.exp(scores - jnp.max(scores, axis=2, keepdims=True))
    probabilities = (shifted / jnp.sum(shifted, axis=2, keepdims=True)).astype(jnp.bfloat16)
    attended = jnp.einsum(
        "rgp,rpd->rgd", probabilities, values[:, 0], preferred_element_type=jnp.float32
    )
    return attended.astype(jnp.bfloat16).reshape(rows, group * width)


def expert_rows(rows, weight_gate_up, weight_down):
    hidden_units = weight_down.shape[0]
    both = jnp.dot(rows, weight_gate_up, preferred_element_type=jnp.float32)
    active = (jax.nn.silu(both[:, :hidden_units]) * both[:, hidden_units:]).astype(jnp.bfloat16)
    return jnp.dot(active, weight_down, preferred_element_type=jnp.float32).astype(jnp.bfloat16)


def route_targets(routes, experts, capacity):
    flat = routes.reshape(-1)
    hits = (flat[:, None] == lax.broadcasted_iota(jnp.int32, (flat.shape[0], experts), 1)).astype(
        jnp.int32
    )
    slot = jnp.sum(hits * (jnp.cumsum(hits, axis=0) - 1), axis=1)
    return flat * capacity + slot


def body(
    queries,
    keys,
    values,
    lengths,
    o_proj,
    residual,
    norm_gain,
    gate_up,
    down,
    routes,
    route_weights,
):
    req_count = lax.axis_size("req")
    group_count = lax.axis_size("kvh")
    tok_src = residual.shape[0]
    model_width = residual.shape[1]
    attended = attend(queries, keys, values, lengths)
    partial_columns = jnp.dot(
        lax.all_gather(attended, "req", axis=0, tiled=True),
        o_proj,
        preferred_element_type=jnp.float32,
    )
    columns = partial_columns.shape[1]
    ordered = (
        partial_columns.reshape(req_count, group_count, tok_src, columns)
        .transpose(1, 0, 2, 3)
        .reshape(-1, columns)
    )
    summed = lax.psum_scatter(ordered, "kvh", scatter_dimension=0, tiled=True)
    projected = lax.all_to_all(summed, "req", split_axis=0, concat_axis=1, tiled=True)
    state = residual.astype(jnp.float32) + projected
    factor = lax.rsqrt(jnp.mean(state * state, axis=1, keepdims=True) + 1e-06)
    normed = (state * factor * norm_gain).astype(jnp.bfloat16)
    experts = req_count * group_count
    route_count = routes.shape[1]
    capacity = min(tok_src, max(2, (tok_src * route_count + experts - 1) // experts + 1))
    targets = route_targets(routes, experts, capacity)
    table = (
        lax.broadcasted_iota(jnp.int32, (experts * capacity, targets.shape[0]), 0)
        == targets[None, :]
    )
    table = jnp.any(table.reshape(experts * capacity, tok_src, route_count), axis=2).astype(
        jnp.bfloat16
    )
    outgoing = jnp.dot(table, normed, preferred_element_type=jnp.float32).astype(jnp.bfloat16)
    local_gate_up = gate_up[0]
    local_down = down[0]
    received = lax.all_to_all(
        outgoing.reshape(experts, capacity, model_width),
        ("req", "kvh"),
        split_axis=0,
        concat_axis=0,
        tiled=True,
    )
    result = expert_rows(received.reshape(-1, model_width), local_gate_up, local_down)
    returned = lax.all_to_all(
        result.reshape(received.shape), ("req", "kvh"), split_axis=0, concat_axis=0, tiled=True
    )
    picked = returned.reshape(experts * capacity, model_width)[targets]
    blended = jnp.sum(
        picked.reshape(tok_src, route_count, model_width).astype(jnp.float32)
        * route_weights[:, :, None],
        axis=1,
    )
    return (state + blended).astype(jnp.bfloat16)


def solution(mesh):
    in_specs = (
        P("req", "kvh"),
        P("req", "kvh", None, None),
        P("req", "kvh", None, None),
        P("req"),
        P("kvh", "req"),
        P(("req", "kvh"), None),
        P(),
        P(("req", "kvh"), None, None),
        P(("req", "kvh"), None, None),
        P(("req", "kvh"), None),
        P(("req", "kvh"), None),
    )
    out_specs = P(("req", "kvh"), None)
    return jax.shard_map(body, mesh=mesh, in_specs=in_specs, out_specs=out_specs, check_vma=False)
```

profile of v0, /device:TPU:1, one launch (start us, length us, event | category | flops | bytes accessed | tf_op | source)
XLA Modules:
  0.0 274.9 jit_solution(1444735004367407012)
XLA Ops:
  6.5 0.0 copy-start
  6.5 0.0 all-gather.2.cloned.1.call-start
  6.5 1.1 copy.29
  7.6 0.7 iota_compare_fusion.2
  8.4 0.0 copy-done
  8.4 1.3 fusion.18
  9.7 0.3 fusion.36
  10.0 3.0 %fusion.21 = bf16[48,16,128]{2,1,0:T(8,128)(2,1)S(1)} fusion(bf16[48,1,192,128]{3,2,1,0:T(8,128)(2,1)} %param.13, f32[48,16]{1,0:T(8,128)S(1)} %fusion.36, f32[48,16,192]{2,1,0:T(8,128)S(1)} %fusion.18), kind=kOutput, calls=%fused_computation.18 | convolution fusion | flops 38290368 | bytes 3148800 | tf_op jit(solution)/shard_map/rgp,rpd->rgd/dot_general | solution.py:21
  13.1 0.7 copy.33
  13.8 0.0 all-gather.2.cloned.1.call-update
  13.8 0.0 reduce-scatter.2.cloned.1.call-start
  13.9 94.8 %all-gather.2.cloned.1.call-done = bf16[1536,2048]{1,0:T(8,128)(2,1)} async-done(((bf16[48,2048]{1,0:T(8,128)(2,1)}), bf16[1536,2048]{1,0:T(8,128)(2,1)}) %all-gather.2.cloned.1.call-update) | async-done | bytes 6291472 | tf_op jit(solution)/shard_map/all_gather | solution.py:62
  108.7 5.5 %fusion.37 = f32[1536,128]{1,0:T(8,128)} fusion(bf16[1536,2048]{1,0:T(8,128)(2,1)} %all-gather.2.cloned.1.call-done, bf16[2048,128]{1,0:T(8,128)(2,1)} %param.15), kind=kOutput, calls=%fused_computation.47 | convolution fusion | flops 805306368 | bytes 7602176 | tf_op jit(solution)/shard_map/dot_general | solution.py:61
  114.2 1.2 reshape.104
  115.4 0.0 copy-start.3
  115.5 1.1 copy.24
  116.5 2.3 reshape.105
  118.8 0.0 reduce-scatter.2.cloned.1.call-update
  118.8 0.1 copy.26
  118.9 0.1 eq.19
  119.0 0.1 fusion.31
  119.1 0.1 reduce_window_sum.11
  119.2 0.2 select_reduce_fusion
  119.4 0.1 reduce_sum.42
  119.5 17.4 %reduce-scatter.2.cloned.1.call-done = f32[384,128]{1,0:T(8,128)} async-done(((f32[1536,128]{1,0:T(8,128)}), f32[384,128]{1,0:T(8,128)}) %reduce-scatter.2.cloned.1.call-update) | async-done | bytes 196624 | tf_op jit(solution)/shard_map/reduce_scatter | solution.py:72
  136.9 1.6 all_to_all.20
  138.6 9.2 %all-to-all-start = ((f32[32,12,128]{2,1,0:T(8,128)}), f32[32,12,128]{2,1,0:T(8,128)S(1)}, u32[]{:S(2)}, u32[]{:S(2)}) async-start(f32[32,12,128]{2,1,0:T(8,128)} %all_to_all.20), calls=%async_computation.1 | async-start | bytes 524288 | tf_op jit(solution)/shard_map/all_to_all | solution.py:73
  147.8 0.1 fusion.30
  147.9 10.3 %all-to-all-done = f32[32,12,128]{2,1,0:T(8,128)S(1)} async-done(((f32[32,12,128]{2,1,0:T(8,128)}), f32[32,12,128]{2,1,0:T(8,128)S(1)}, u32[]{:S(2)}, u32[]{:S(2)}) %all-to-all-start) | async-done | bytes 196640 | tf_op jit(solution)/shard_map/all_to_all | solution.py:73
  158.2 0.1 copy.25
  158.3 0.2 copy.31
  158.5 0.0 copy-done.1
  158.5 0.2 multiply_reduce_fusion
  158.7 2.0 convolution_convert_fusion
  160.7 4.4 %reshape.106 = bf16[128,2,4096]{2,1,0:T(2,128)(2,1)} reshape(bf16[256,4096]{1,0:T(8,128)(2,1)} %convolution_convert_fusion) | data formatting | bytes 4194304 | tf_op jit(solution)/shard_map/reshape | solution.py:92
  165.1 36.5 %all_to_all.29 = bf16[128,2,4096]{2,1,0:T(2,128)(2,1)} all-to-all(bf16[128,2,4096]{2,1,0:T(2,128)(2,1)} %reshape.106), channel_id=1, replica_groups=mesh['req'=32,'kvh'=4] {'req','kvh'}, dimensions={0} | all-to-all | bytes 4194304 | tf_op jit(solution)/shard_map/all_to_all | solution.py:91
  201.6 4.1 %reshape.107 = bf16[256,4096]{1,0:T(8,128)(2,1)} reshape(bf16[128,2,4096]{2,1,0:T(2,128)(2,1)} %all_to_all.29) | data formatting | bytes 4194304 | tf_op jit(solution)/shard_map/reshape | solution.py:98
  205.7 7.0 %fusion.1 = f32[256,1536]{1,0:T(8,128)S(1)} fusion(bf16[256,4096]{1,0:T(8,128)(2,1)} %reshape.107, bf16[1,4096,1536]{2,1,0:T(8,128)(2,1)} %param.18), kind=kOutput, calls=%fused_computation.2 | convolution fusion | flops 3221225472 | bytes 16252928 | tf_op jit(solution)/shard_map/dot_general | solution.py:29
  212.7 6.0 %fusion.5 = bf16[256,4096]{1,0:T(8,128)(2,1)} fusion(bf16[1,768,4096]{2,1,0:T(8,128)(2,1)} %param.19, f32[256,1536]{1,0:T(8,128)S(1)} %fusion.1), kind=kOutput, calls=%fused_computation.7 | convolution fusion | flops 1612840960 | bytes 9961472 | tf_op jit(solution)/shard_map/dot_general | solution.py:31
  218.7 4.4 %reshape.108 = bf16[128,2,4096]{2,1,0:T(2,128)(2,1)} reshape(bf16[256,4096]{1,0:T(8,128)(2,1)} %fusion.5) | data formatting | bytes 4194304 | tf_op jit(solution)/shard_map/reshape | solution.py:100
  223.1 5.6 %all-to-all-start.2 = ((bf16[128,2,4096]{2,1,0:T(2,128)(2,1)}), bf16[128,2,4096]{2,1,0:T(2,128)(2,1)}, u32[]{:S(2)}, u32[]{:S(2)}) async-start(bf16[128,2,4096]{2,1,0:T(2,128)(2,1)} %reshape.108), calls=%async_computation.3 | async-start | bytes 4194304 | tf_op jit(solution)/shard_map/all_to_all | solution.py:99
  228.7 0.1 mul.67
  228.8 0.1 copy.28
  228.9 30.1 %all-to-all-done.2 = bf16[128,2,4096]{2,1,0:T(2,128)(2,1)} async-done(((bf16[128,2,4096]{2,1,0:T(2,128)(2,1)}), bf16[128,2,4096]{2,1,0:T(2,128)(2,1)}, u32[]{:S(2)}, u32[]{:S(2)}) %all-to-all-start.2) | async-done | bytes 2097184 | tf_op jit(solution)/shard_map/all_to_all | solution.py:99
  259.0 4.1 %reshape.109 = bf16[256,4096]{1,0:T(8,128)(2,1)} reshape(bf16[128,2,4096]{2,1,0:T(2,128)(2,1)} %all-to-all-done.2) | data formatting | bytes 4194304 | tf_op jit(solution)/shard_map/reshape | solution.py:102
  263.1 3.6 %gather_fusion = bf16[96,4096]{1,0:T(8,128)(2,1)S(1)} fusion(bf16[256,4096]{1,0:T(8,128)(2,1)} %reshape.109, s32[1024]{0:T(1024)S(1)} %pad_clamp_fusion), kind=kCustom, calls=%fused_computation | custom fusion | bytes 1573248 | tf_op jit(solution)/shard_map/gather | solution.py:102
  266.8 0.6 fusion.12
  267.4 0.7 add_convert_fusion
  (11 shorter events, 0.1 us)
Async XLA Ops:
  6.5 1.9 copy-start
  6.5 102.2 %all-gather.2.cloned.1.call-start = ((), (), s32[]{:S(2)}) async-start(), calls=%async_computation.4 | async-start | bytes 6488064 | tf_op jit(solution)/shard_map/all_gather | solution.py:62
  13.8 123.1 %reduce-scatter.2.cloned.1.call-start = ((), (), s32[]{:S(2)}) async-start(), calls=%async_computation.5 | async-start | bytes 983040 | tf_op jit(solution)/shard_map/reduce_scatter | solution.py:72
  115.4 3.4 %copy-start.3 = (s32[12,8]{0,1:T(8,128)S(1)}, s32[12,8]{0,1:T(8,128)}, u32[]{:S(2)}) copy-start(s32[12,8]{0,1:T(8,128)} %param.20) | copy-start | bytes 1156
  116.5 41.9 %copy-start.1 = (bf16[12,4096]{1,0:T(8,128)(2,1)S(1)}, bf16[12,4096]{1,0:T(8,128)(2,1)}, u32[]{:S(2)}) copy-start(bf16[12,4096]{1,0:T(8,128)(2,1)} %param.16) | copy-start | bytes 294916
  118.8 39.9 %copy-start.2 = (f32[4096]{0:T(1024)S(1)}, f32[4096]{0:T(1024)}, u32[]{:S(2)}) copy-start(f32[4096]{0:T(1024)} %param.17) | copy-start | bytes 49156
  138.6 19.7 %all-to-all-start = ((f32[32,12,128]{2,1,0:T(8,128)}), f32[32,12,128]{2,1,0:T(8,128)S(1)}, u32[]{:S(2)}, u32[]{:S(2)}) async-start(f32[32,12,128]{2,1,0:T(8,128)} %all_to_all.20), calls=%async_computation.1 | async-start | bytes 524288 | tf_op jit(solution)/shard_map/all_to_all | solution.py:73
  223.1 5.7 %copy-start.4 = (f32[12,8]{0,1:T(8,128)S(1)}, f32[12,8]{0,1:T(8,128)}, u32[]{:S(2)}) copy-start(f32[12,8]{0,1:T(8,128)} %param.21) | copy-start | bytes 1156
  223.1 35.9 %all-to-all-start.2 = ((bf16[128,2,4096]{2,1,0:T(2,128)(2,1)}), bf16[128,2,4096]{2,1,0:T(2,128)(2,1)}, u32[]{:S(2)}, u32[]{:S(2)}) async-start(bf16[128,2,4096]{2,1,0:T(2,128)(2,1)} %reshape.108), calls=%async_computation.3 | async-start | bytes 4194304 | tf_op jit(solution)/shard_map/all_to_all | solution.py:99
Sparse Core Ops, SparseCore 0:
  13.9 94.7 all-gather.1
  118.9 17.9 reduce-scatter.1
where the time goes:
time: 276 us; the launch traced here: 275 us
  waiting for transfers between devices  153 us (55%)
  blocking collectives  36.5 us (13%)
  local copies, waits for them, and re-layouts  29.4 us (11%)
  matrix products  25 us (9%)
  starting transfers between devices  14.8 us (5%)
  between operations  13.6 us (5%)
  other arithmetic  3.04 us (1%)
    all_gather x1, waiting for transfers between devices, body(): lax.all_gather(attended, 'req', axis=0, tiled=True)  94.8 us
    all_to_all x1, blocking collectives, body(): lax.all_to_all(outgoing.reshape(experts, capacity, model_width), ('req',...  36.5 us
    all_to_all x1, waiting for transfers between devices, body(): lax.all_to_all(result.reshape(received.shape), ('req', 'kvh'), split_axis...  30.1 us
    reduce_scatter x1, waiting for transfers between devices, body(): summed = lax.psum_scatter(ordered, 'kvh', scatter_dimension=0, tiled=True)  17.4 us
    all_to_all x1, waiting for transfers between devices, body(): lax.all_to_all(summed, 'req', split_axis=0, concat_axis=1, tiled=True)  10.3 us
    all_to_all x1, starting transfers between devices, body(): lax.all_to_all(summed, 'req', split_axis=0, concat_axis=1, tiled=True)  9.18 us
    dot_general x1, matrix products, expert_rows(): both = jnp.dot(rows, weight_gate_up, preferred_element_type=jnp.float32)  7.02 us
    dot_general x1, matrix products, expert_rows(): jnp.dot(active, weight_down, preferred_element_type=jnp.float32)  6.01 us
  transfers between devices with their start and end apart: 4, of which 4 were waited for; matrix products, arithmetic and copies ran while one was open for 0% of the time, Pallas kernels for 0%

commit v1 on v0

v1 whole, which is shorter than its diff:
```python
import math

import jax
import jax.numpy as jnp
from jax import lax
from jax.sharding import PartitionSpec as P
from jax.experimental import pallas as pl
from jax.experimental.pallas import tpu as pltpu

K_STEP = 37
K_INV = 45
N_DEV = 128
MESH = pl.DeviceIdType.MESH


def coords():
    r = lax.axis_index("req")
    k = lax.axis_index("kvh")
    return lax.rem(r, 2) * 2 + k // 2, r // 8, lax.rem(r // 2, 4), lax.rem(k, 2)


def place(x, y, z, c):
    x, y, z, c = lax.rem(x, 4), lax.rem(y, 4), lax.rem(z, 4), lax.rem(c, 2)
    return ((y * 4 + z) * 2 + x // 2, lax.rem(x, 2) * 2 + c)


def enter(along_y, along_z):
    x, y, z, c = coords()
    barrier = pltpu.get_barrier_semaphore()
    for dx in range(4):
        for dc in range(2):
            if dx or dc:
                pl.semaphore_signal(barrier, inc=1, device_id=place(x + dx, y, z, c + dc), device_id_type=MESH)
    for d in range(1, 4):
        pl.semaphore_signal(barrier, inc=1, device_id=place(x, y + d, z, c), device_id_type=MESH)
        pl.semaphore_signal(barrier, inc=1, device_id=place(x, y, z + d, c), device_id_type=MESH)
    pl.semaphore_wait(barrier, 13)
    for d in range(1, 4):
        pl.semaphore_signal(along_y, inc=1, device_id=place(x, y + d, z, c), device_id_type=MESH)
    pl.semaphore_wait(along_y, 3)
    for d in range(1, 4):
        pl.semaphore_signal(along_z, inc=1, device_id=place(x, y, z + d, c), device_id_type=MESH)
    pl.semaphore_wait(along_z, 3)


def iota(shape, dim):
    return lax.broadcasted_iota(jnp.int32, shape, dim)


def route_keys(expert, token, routes_smem, me):
    slot = jnp.zeros_like(expert)
    for t in range(12):
        for k in range(8):
            slot = slot + jnp.where((expert == routes_smem[t, k]) & (token > t), 1, 0)
    key = (((expert - me + N_DEV) * K_INV) & (N_DEV - 1)) * 2 + slot
    return jnp.where(token < 12, key, -1)


def expert_kernel(
    state_ref, gain_ref, routes_smem, routes_ref, weights_ref, gate_up_hbm, down_hbm,
    out_ref,
    gate_up, down, sent, received, rows, active, permuted, results, returned, normed, mix,
    weight_sem, send_sem, recv_sem, back_sem, return_sem, along_y, along_z,
):
    me = lax.axis_index("req") * 4 + lax.axis_index("kvh")
    bf16, f32 = jnp.bfloat16, jnp.float32
    loads = [
        pltpu.make_async_copy(gate_up_hbm, gate_up, weight_sem.at[0]),
        pltpu.make_async_copy(down_hbm, down, weight_sem.at[1]),
    ]
    for load in loads:
        load.start()
    enter(along_y, along_z)

    state = state_ref[...]
    factor = lax.rsqrt(jnp.sum(state * state, axis=1, keepdims=True) * (1.0 / 4096.0) + 1e-06)
    scaled = (state * factor * gain_ref[...]).astype(bf16)
    for s in range(8):
        normed[s * 16 : (s + 1) * 16, :] = scaled[:, s * 512 : (s + 1) * 512]

    lane = iota((8, 128), 1)
    sub = iota((8, 128), 0)
    token = lane & 15
    expert = jnp.full((8, 128), -1, jnp.int32)
    for t in range(12):
        for k in range(8):
            expert = jnp.where((sub == k) & (token == t), routes_smem[t, k], expert)
    keys = route_keys(expert, token, routes_smem, me)
    for part in range(8):
        row = iota((256, 128), 0) + part * 256
        hit = jnp.zeros((256, 128), f32)
        for k in range(8):
            hit = jnp.where(row // 8 == keys[k : k + 1, :], 1.0, hit)
        table = jnp.where((row & 7) == iota((256, 128), 1) // 16, hit, 0.0).astype(bf16)
        block = jnp.dot(table, normed[...], preferred_element_type=f32).astype(bf16)
        sent[part * 16 : (part + 1) * 16] = block.reshape(16, 16, 512)

    def send(d, carry):
        to = lax.rem(me + d * K_STEP, N_DEV)
        group = d // 64
        pltpu.make_async_remote_copy(
            src_ref=sent.at[d], dst_ref=received.at[d], send_sem=send_sem.at[group],
            recv_sem=recv_sem.at[group], device_id=(to // 4, lax.rem(to, 4)), device_id_type=MESH,
        ).start()
        return carry

    lax.fori_loop(1, N_DEV, send, 0)
    received[0] = sent[0]

    expert_column = jnp.concatenate([routes_ref[...]] * 8, axis=0)
    token_column = iota((128, 8), 0) & 15
    key_column = route_keys(expert_column, token_column, routes_smem, me)
    gates = jnp.concatenate([weights_ref[...]] * 8, axis=0)
    for part in range(8):
        column = iota((128, 256), 1) + part * 256
        share = jnp.zeros((128, 256), f32)
        for k in range(8):
            share = jnp.where(column // 8 == key_column[:, k : k + 1], gates[:, k : k + 1], share)
        share = jnp.where((column & 7) == iota((128, 256), 0) // 16, share, 0.0)
        high = share.astype(bf16)
        mix[:128, part * 256 : (part + 1) * 256] = high
        mix[128:, part * 256 : (part + 1) * 256] = (share - high.astype(f32)).astype(bf16)

    i, j = iota((256, 256), 0), iota((256, 256), 1)
    spread = jnp.where(j == (i & 31) * 8 + i // 32, 1.0, 0.0).astype(bf16)
    gather = jnp.where(i == (j & 31) * 8 + j // 32, 1.0, 0.0).astype(bf16)

    for group in range(2):
        first = 1 if group == 0 else 64
        landed = received.at[pl.ds(first, 64 * (group + 1) - first)]
        pltpu.make_async_copy(landed, landed, recv_sem.at[group]).wait()
        for chunk in range(4):
            block = received[group * 64 + chunk * 16 : group * 64 + (chunk + 1) * 16].reshape(256, 512)
            block = jnp.dot(spread, block, preferred_element_type=f32).astype(bf16)
            for s in range(8):
                rows[chunk * 32 : (chunk + 1) * 32, s * 512 : (s + 1) * 512] = block[s * 32 : (s + 1) * 32]
        if group == 0:
            loads[0].wait()
        for n in range(3):
            gate = jnp.dot(rows[...], gate_up[:, n * 256 : (n + 1) * 256], preferred_element_type=f32)
            up = jnp.dot(rows[...], gate_up[:, 768 + n * 256 : 768 + (n + 1) * 256], preferred_element_type=f32)
            active[:, n * 256 : (n + 1) * 256] = (gate / (1.0 + jnp.exp(-gate)) * up).astype(bf16)
        if group == 0:
            loads[1].wait()
        for s in range(8):
            part = jnp.dot(active[...], down[:, s * 512 : (s + 1) * 512], preferred_element_type=f32).astype(bf16)
            for chunk in range(4):
                permuted[chunk, s * 32 : (s + 1) * 32, :] = part[chunk * 32 : (chunk + 1) * 32]
        for chunk in range(4):
            block = jnp.dot(gather, permuted[chunk], preferred_element_type=f32).astype(bf16)
            results[group * 64 + chunk * 16 : group * 64 + (chunk + 1) * 16] = block.reshape(16, 16, 512)

        def send_back(d, carry):
            to = lax.rem(me + N_DEV * K_STEP - d * K_STEP, N_DEV)
            pltpu.make_async_remote_copy(
                src_ref=results.at[d], dst_ref=returned.at[d], send_sem=back_sem.at[0],
                recv_sem=return_sem.at[0], device_id=(to // 4, lax.rem(to, 4)), device_id_type=MESH,
            ).start()
            return carry

        lax.fori_loop(first, 64 * (group + 1), send_back, 0)
        if group == 0:
            returned[0] = results[0]

    landed = returned.at[pl.ds(1, 127)]
    pltpu.make_async_copy(landed, landed, return_sem.at[0]).wait()
    both = jnp.dot(mix[...], returned[...].reshape(2048, 512), preferred_element_type=f32)
    blended = both[:128] + both[128:]
    for s in range(8):
        columns = slice(s * 512, (s + 1) * 512)
        total = state_ref[:, columns] + blended[s * 16 : (s + 1) * 16]
        out_ref[:, columns] = total[:12].astype(bf16)
    gone = sent.at[pl.ds(1, 63)]
    pltpu.make_async_copy(gone, gone, send_sem.at[0]).wait()
    gone = sent.at[pl.ds(64, 64)]
    pltpu.make_async_copy(gone, gone, send_sem.at[1]).wait()
    gone = results.at[pl.ds(1, 127)]
    pltpu.make_async_copy(gone, gone, back_sem.at[0]).wait()


def experts(state, gain, routes, weights, gate_up, down):
    bf16, f32 = jnp.bfloat16, jnp.float32
    vmem = pl.BlockSpec(memory_space=pltpu.VMEM)
    smem = pl.BlockSpec(memory_space=pltpu.SMEM)
    hbm = pl.BlockSpec(memory_space=pl.ANY)
    pad = lambda a: jnp.pad(a, ((0, 4), (0, 0)))
    return pl.pallas_call(
        expert_kernel,
        out_shape=jax.ShapeDtypeStruct((12, 4096), bf16),
        in_specs=[vmem, vmem, smem, vmem, vmem, hbm, hbm],
        out_specs=vmem,
        scratch_shapes=[
            pltpu.VMEM((4096, 1536), bf16),
            pltpu.VMEM((768, 4096), bf16),
            pltpu.VMEM((128, 16, 512), bf16),
            pltpu.VMEM((128, 16, 512), bf16),
            pltpu.VMEM((128, 4096), bf16),
            pltpu.VMEM((128, 768), bf16),
            pltpu.VMEM((4, 256, 512), bf16),
            pltpu.VMEM((128, 16, 512), bf16),
            pltpu.VMEM((128, 16, 512), bf16),
            pltpu.VMEM((128, 512), bf16),
            pltpu.VMEM((256, 2048), bf16),
            pltpu.SemaphoreType.DMA((2,)),
            pltpu.SemaphoreType.DMA((2,)),
            pltpu.SemaphoreType.DMA((2,)),
            pltpu.SemaphoreType.DMA((1,)),
            pltpu.SemaphoreType.DMA((1,)),
            pltpu.SemaphoreType.REGULAR,
            pltpu.SemaphoreType.REGULAR,
        ],
        compiler_params=pltpu.CompilerParams(
            collective_id=1, has_side_effects=True, vmem_limit_bytes=56 * 2**20
        ),
        cost_estimate=pl.CostEstimate(flops=6 * 10**9, bytes_accessed=2 * 10**7, transcendentals=10**6),
        name="experts",
    )(pad(state), gain[None, :], routes, pad(routes), pad(weights), gate_up, down)


def attend(queries, keys, values, lengths):
    rows = queries.shape[0]
    width = keys.shape[3]
    group = queries.shape[1] // width
    query_heads = queries.reshape(rows, group, width)
    scores = jnp.einsum(
        "rgd,rpd->rgp", query_heads, keys[:, 0], preferred_element_type=jnp.float32
    ) / math.sqrt(width)
    valid = lax.broadcasted_iota(jnp.int32, (rows, keys.shape[2]), 1) < lengths[:, None]
    scores = jnp.where(valid[:, None, :], scores, -1e30)
    shifted = jnp.exp(scores - jnp.max(scores, axis=2, keepdims=True))
    probabilities = (shifted / jnp.sum(shifted, axis=2, keepdims=True)).astype(jnp.bfloat16)
    attended = jnp.einsum(
        "rgp,rpd->rgd", probabilities, values[:, 0], preferred_element_type=jnp.float32
    )
    return attended.astype(jnp.bfloat16).reshape(rows, group * width)


def body(
    queries,
    keys,
    values,
    lengths,
    o_proj,
    residual,
    norm_gain,
    gate_up,
    down,
    routes,
    route_weights,
):
    req_count = lax.axis_size("req")
    group_count = lax.axis_size("kvh")
    tok_src = residual.shape[0]
    attended = attend(queries, keys, values, lengths)
    partial_columns = jnp.dot(
        lax.all_gather(attended, "req", axis=0, tiled=True),
        o_proj,
        preferred_element_type=jnp.float32,
    )
    columns = partial_columns.shape[1]
    ordered = (
        partial_columns.reshape(req_count, group_count, tok_src, columns)
        .transpose(1, 0, 2, 3)
        .reshape(-1, columns)
    )
    summed = lax.psum_scatter(ordered, "kvh", scatter_dimension=0, tiled=True)
    projected = lax.all_to_all(summed, "req", split_axis=0, concat_axis=1, tiled=True)
    state = residual.astype(jnp.float32) + projected
    return experts(state, norm_gain, routes, route_weights, gate_up[0], down[0])


def solution(mesh):
    in_specs = (
        P("req", "kvh"),
        P("req", "kvh", None, None),
        P("req", "kvh", None, None),
        P("req"),
        P("kvh", "req"),
        P(("req", "kvh"), None),
        P(),
        P(("req", "kvh"), None, None),
        P(("req", "kvh"), None, None),
        P(("req", "kvh"), None),
        P(("req", "kvh"), None),
    )
    out_specs = P(("req", "kvh"), None)
    return jax.shard_map(body, mesh=mesh, in_specs=in_specs, out_specs=out_specs, check_vma=False)
```

time: 276 us -> 227 us (0.82)
  Pallas kernels: 0 us -> 59 us
  blocking collectives: 36.5 us -> 0 us
  waiting for transfers between devices: 153 us -> 122 us
  local copies, waits for them, and re-layouts: 29.4 us -> 11.9 us
  matrix products: 25 us -> 9.9 us
  starting transfers between devices: 14.8 us -> 9.41 us
    pallas_call x0 -> x1, Pallas kernels: none -> 59 us  [experts(): pl.pallas_call(expert_kernel, out_shape=jax.ShapeDtypeStruct((12, 4096),...]
    all_to_all x1 -> x0, blocking collectives: 36.5 us -> none  [body(): lax.all_to_all(outgoing.reshape(experts, capacity, model_width), ('req',...]
    all_to_all x1 -> x0, waiting for transfers between devices: 30.1 us -> none  [body(): lax.all_to_all(result.reshape(received.shape), ('req', 'kvh'), split_axis...]
    reshape x4 -> x0, local copies, waits for them, and re-layouts: 17 us -> none  [the longest x1 4.4 us: body(): result.reshape(received.shape)]
    dot_general x3 -> x0, matrix products: 15.1 us -> none  [the longest x1 7.02 us: expert_rows(): both = jnp.dot(rows, weight_gate_up, preferred_element_type=jnp.float32)]
    all_to_all x1 -> x0, starting transfers between devices: 5.57 us -> none  [body(): lax.all_to_all(result.reshape(received.shape), ('req', 'kvh'), split_axis...]
    gather x1 -> x0, local copies, waits for them, and re-layouts: 3.65 us -> none  [body(): picked = returned.reshape(experts * capacity, model_width)[targets]]
  transfers between devices with their start and end apart: 4 -> 3, of which waited for: 4 -> 3; matrix products, arithmetic and copies ran while one was open for 0% -> 1% of each run, Pallas kernels for 0% -> 0%
where the time goes in v1:
time: 227 us
  waiting for transfers between devices  122 us (54%)
  Pallas kernels  59 us (26%)
  between operations  13.5 us (6%)
  local copies, waits for them, and re-layouts  11.9 us (5%)
  matrix products  9.9 us (4%)
  starting transfers between devices  9.41 us (4%)
    all_gather x1, waiting for transfers between devices, body(): lax.all_gather(attended, 'req', axis=0, tiled=True)  94.8 us
    pallas_call x1, Pallas kernels, experts(): pl.pallas_call(expert_kernel, out_shape=jax.ShapeDtypeStruct((12, 4096),...  59 us
    reduce_scatter x1, waiting for transfers between devices, body(): summed = lax.psum_scatter(ordered, 'kvh', scatter_dimension=0, tiled=True)  18.1 us
    all_to_all x1, starting transfers between devices, body(): lax.all_to_all(summed, 'req', split_axis=0, concat_axis=1, tiled=True)  9.37 us
    all_to_all x1, waiting for transfers between devices, body(): lax.all_to_all(summed, 'req', split_axis=0, concat_axis=1, tiled=True)  8.9 us
    dot_general x1, matrix products, body(): jnp.dot(lax.all_gather(attended, 'req', axis=0, tiled=True), o_proj, pref...  5.53 us
  transfers between devices with their start and end apart: 3, of which 3 were waited for; matrix products, arithmetic and copies ran while one was open for 1% of the time, Pallas kernels for 0%

profile of v1, /device:TPU:1, one launch (start us, length us, event | category | flops | bytes accessed | tf_op | source)
XLA Modules:
  0.0 226.7 jit_solution(1557747509258520995)
XLA Ops:
  6.5 0.0 copy-start
  6.5 0.0 all-gather.2.cloned.1.call-start
  6.5 1.1 copy.20
  7.6 0.7 iota_compare_fusion
  8.4 0.0 copy-done
  8.4 1.3 fusion.10
  9.7 0.3 fusion.18
  10.0 3.0 %fusion.13 = bf16[48,16,128]{2,1,0:T(8,128)(2,1)S(1)} fusion(bf16[48,1,192,128]{3,2,1,0:T(8,128)(2,1)} %param.13, f32[48,16]{1,0:T(8,128)S(1)} %fusion.18, f32[48,16,192]{2,1,0:T(8,128)S(1)} %fusion.10), kind=kOutput, calls=%fused_computation.9 | convolution fusion | flops 38290368 | bytes 3148800 | tf_op jit(solution)/shard_map/rgp,rpd->rgd/dot_general | solution.py:232
  13.1 0.7 copy.24
  13.8 0.0 all-gather.2.cloned.1.call-update
  13.8 0.0 reduce-scatter.2.cloned.1.call-start
  13.9 94.8 %all-gather.2.cloned.1.call-done = bf16[1536,2048]{1,0:T(8,128)(2,1)} async-done(((bf16[48,2048]{1,0:T(8,128)(2,1)}), bf16[1536,2048]{1,0:T(8,128)(2,1)}) %all-gather.2.cloned.1.call-update) | async-done | bytes 6291472 | tf_op jit(solution)/shard_map/all_gather | solution.py:256
  108.7 5.5 %fusion.19 = f32[1536,128]{1,0:T(8,128)} fusion(bf16[1536,2048]{1,0:T(8,128)(2,1)} %all-gather.2.cloned.1.call-done, bf16[2048,128]{1,0:T(8,128)(2,1)} %param.15), kind=kOutput, calls=%fused_computation.17 | convolution fusion | flops 805306368 | bytes 7602176 | tf_op jit(solution)/shard_map/dot_general | solution.py:255
  114.2 1.2 reshape.34
  115.4 0.0 copy-start.3
  115.5 0.0 copy-start.4
  115.5 1.1 copy.15
  116.5 0.0 copy-start.1
  116.5 2.2 reshape.35
  118.8 0.0 reduce-scatter.2.cloned.1.call-update
  118.8 18.1 %reduce-scatter.2.cloned.1.call-done = f32[384,128]{1,0:T(8,128)} async-done(((f32[1536,128]{1,0:T(8,128)}), f32[384,128]{1,0:T(8,128)}) %reduce-scatter.2.cloned.1.call-update) | async-done | bytes 196624 | tf_op jit(solution)/shard_map/reduce_scatter | solution.py:266
  136.9 1.6 all_to_all.14
  138.5 9.4 %all-to-all-start = ((f32[32,12,128]{2,1,0:T(8,128)}), f32[32,12,128]{2,1,0:T(8,128)S(1)}, u32[]{:S(2)}, u32[]{:S(2)}) async-start(f32[32,12,128]{2,1,0:T(8,128)} %all_to_all.14), calls=%async_computation.1 | async-start | bytes 524288 | tf_op jit(solution)/shard_map/all_to_all | solution.py:267
  147.9 0.0 copy-done.3
  147.9 0.1 copy.19.routes_smem
  148.0 0.0 copy-done.4
  148.0 0.0 copy-start.2
  148.0 0.1 copy.18
  148.1 0.6 pad.13.routes_ref
  148.7 0.6 pad.14.weights_ref
  149.3 8.9 %all-to-all-done = f32[32,12,128]{2,1,0:T(8,128)S(1)} async-done(((f32[32,12,128]{2,1,0:T(8,128)}), f32[32,12,128]{2,1,0:T(8,128)S(1)}, u32[]{:S(2)}, u32[]{:S(2)}) %all-to-all-start) | async-done | bytes 196640 | tf_op jit(solution)/shard_map/all_to_all | solution.py:267
  158.2 0.1 copy.16
  158.3 0.2 copy.22
  158.5 0.0 copy-done.1
  158.5 0.7 pad.12.state_ref
  159.2 0.0 copy-done.2
  159.2 59.0 %experts.1 = bf16[12,4096]{1,0:T(8,128)(2,1)} custom-call(f32[16,4096]{1,0:T(8,128)} %pad.12.state_ref, f32[1,4096]{1,0:T(1,128)} %bitcast.41, s32[12,8]{1,0:T(8,128)} %copy-done.2, s32[16,8]{1,0:T(8,128)} %pad.13.routes_ref, f32[16,8]{1,0:T(8,128)} %pad.14.weights_ref, bf16[4096,1536]{1,0:T(8,128)(2,1)} %bitcast.39, bf16[768,4096]{1,0:T(8,128)(2,1)} %bitcast.40), custom_call_target="tpu_custom_call" | custom-call | flops 6000000000 | bytes 20000000 | tf_op jit(solution)/shard_map/experts/pallas_call | solution.py:187
  218.2 1.6 copy.26
  (2 shorter events, 0.1 us)
Async XLA Ops:
  6.5 1.9 copy-start
  6.5 102.2 %all-gather.2.cloned.1.call-start = ((), (), s32[]{:S(2)}) async-start(), calls=%async_computation.2 | async-start | bytes 6488064 | tf_op jit(solution)/shard_map/all_gather | solution.py:256
  13.8 123.1 %reduce-scatter.2.cloned.1.call-start = ((), (), s32[]{:S(2)}) async-start(), calls=%async_computation.3 | async-start | bytes 983040 | tf_op jit(solution)/shard_map/reduce_scatter | solution.py:266
  115.4 32.5 %copy-start.3 = (s32[12,8]{0,1:T(8,128)S(1)}, s32[12,8]{0,1:T(8,128)}, u32[]{:S(2)}) copy-start(s32[12,8]{0,1:T(8,128)} %param.20) | copy-start | bytes 1156
  115.5 32.6 %copy-start.4 = (f32[12,8]{0,1:T(8,128)S(1)}, f32[12,8]{0,1:T(8,128)}, u32[]{:S(2)}) copy-start(f32[12,8]{0,1:T(8,128)} %param.21) | copy-start | bytes 1156
  116.5 41.9 %copy-start.1 = (bf16[12,4096]{1,0:T(8,128)(2,1)S(1)}, bf16[12,4096]{1,0:T(8,128)(2,1)}, u32[]{:S(2)}) copy-start(bf16[12,4096]{1,0:T(8,128)(2,1)} %param.16) | copy-start | bytes 294916
  138.5 19.7 %all-to-all-start = ((f32[32,12,128]{2,1,0:T(8,128)}), f32[32,12,128]{2,1,0:T(8,128)S(1)}, u32[]{:S(2)}, u32[]{:S(2)}) async-start(f32[32,12,128]{2,1,0:T(8,128)} %all_to_all.14), calls=%async_computation.1 | async-start | bytes 524288 | tf_op jit(solution)/shard_map/all_to_all | solution.py:267
  148.0 11.2 %copy-start.2 = (s32[12,8]{1,0:T(8,128)}, s32[12,8]{1,0:T(8,128)S(1)}, u32[]{:S(2)}) copy-start(s32[12,8]{1,0:T(8,128)S(1)} %copy.19.routes_smem) | copy-start | bytes 1156
Sparse Core Ops, SparseCore 0:
  14.0 94.7 all-gather.1
  118.9 17.9 reduce-scatter.1

commit v2 on v1

v2 whole, which is shorter than its diff:
```python
import math

import jax
import jax.numpy as jnp
from jax import lax
from jax.experimental import pallas as pl
from jax.experimental.pallas import tpu as pltpu
from jax.sharding import PartitionSpec as P


K_STEP = 37
K_INV = 45
N_DEV = 128
MESH = pl.DeviceIdType.MESH


def coords():
    r = lax.axis_index("req")
    k = lax.axis_index("kvh")
    return lax.rem(r, 2) * 2 + k // 2, r // 8, lax.rem(r // 2, 4), lax.rem(k, 2)


def place(x, y, z, c):
    x, y, z, c = lax.rem(x, 4), lax.rem(y, 4), lax.rem(z, 4), lax.rem(c, 2)
    return ((y * 4 + z) * 2 + x // 2, lax.rem(x, 2) * 2 + c)


def iota(shape, dim):
    return lax.broadcasted_iota(jnp.int32, shape, dim)


def route_keys(expert, token, routes_smem, me):
    slot = jnp.zeros_like(expert)
    for t in range(12):
        for k in range(8):
            slot = slot + jnp.where((expert == routes_smem[t, k]) & (token > t), 1, 0)
    key = (((expert - me + N_DEV) * K_INV) & (N_DEV - 1)) * 2 + slot
    return jnp.where(token < 12, key, -1)


def kernel(
    queries_ref, keys_hbm, values_hbm, lengths_smem, o_proj_hbm, residual_ref, gain_ref, routes_smem, routes_ref,
    weights_ref, gate_up_hbm, down_hbm,
    out_ref,
    keys, values, heads, attended, gathered, projection, partial, pieces, collected, state, routes_padded,
    weights_padded, gate_up, down, sent, received, rows, active, permuted, results, returned, normed, mix, table,
    cache_sem, weight_sem, o_own_sem, o_send_sem, o_recv_sem, a_send_sem, a_recv_sem, p_send_sem, p_recv_sem,
    send_sem, recv_sem, back_sem, return_sem, along_y, along_z,
):
    r, kv = lax.axis_index("req"), lax.axis_index("kvh")
    me = r * 4 + kv
    x, y, z, c = coords()
    at = lax.rem(r, 8)
    bf16, f32 = jnp.bfloat16, jnp.float32

    barrier = pltpu.get_barrier_semaphore()
    for dx in range(4):
        for dc in range(2):
            if dx or dc:
                pl.semaphore_signal(barrier, inc=1, device_id=place(x + dx, y, z, c + dc), device_id_type=MESH)
    for d in range(1, 4):
        pl.semaphore_signal(barrier, inc=1, device_id=place(x, y + d, z, c), device_id_type=MESH)
        pl.semaphore_signal(barrier, inc=1, device_id=place(x, y, z + d, c), device_id_type=MESH)

    def cache_load(g, which):
        source, target = ((keys_hbm, keys), (values_hbm, values))[which]
        part = pl.ds(g * 12, 12)
        return pltpu.make_async_copy(source.at[part], target.at[part], cache_sem.at[which, g])

    for g in range(4):
        cache_load(g, 0).start()
        cache_load(g, 1).start()
    o_own = pltpu.make_async_copy(o_proj_hbm, projection.at[:, pl.ds(0, 128)], o_own_sem)
    o_own.start()
    loads = [
        pltpu.make_async_copy(gate_up_hbm, gate_up, weight_sem.at[0]),
        pltpu.make_async_copy(down_hbm, down, weight_sem.at[1]),
    ]
    for load in loads:
        load.start()
    for h in range(16):
        heads[:, h, :] = queries_ref[:, h * 128 : (h + 1) * 128].astype(f32)

    pl.semaphore_wait(barrier, 13)
    for d in range(1, 4):
        pltpu.make_async_remote_copy(
            src_ref=o_proj_hbm, dst_ref=projection.at[:, pl.ds(d * 128, 128)], send_sem=o_send_sem.at[d - 1],
            recv_sem=o_recv_sem, device_id=place(x, y + d, z, c), device_id_type=MESH,
        ).start()
    for d in range(1, 4):
        pl.semaphore_signal(along_y, inc=1, device_id=place(x, y + d, z, c), device_id_type=MESH)

    position = iota((16, 192), 1)

    def attend(g, carry):
        cache_load(g, 0).wait()
        cache_load(g, 1).wait()
        for b in range(12):
            i = g * 12 + b
            scores = lax.dot_general(
                heads[i].astype(bf16), keys[i], (((1,), (1,)), ((), ())), preferred_element_type=f32
            ) * (1.0 / math.sqrt(128.0))
            scores = jnp.where(position < lengths_smem[i], scores, -1e30)
            shifted = jnp.exp(scores - jnp.max(scores, axis=1, keepdims=True))
            shares = (shifted / jnp.sum(shifted, axis=1, keepdims=True)).astype(bf16)
            attended[i] = jnp.dot(shares, values[i], preferred_element_type=f32)
        return carry

    lax.fori_loop(0, 4, attend, 0)
    pl.semaphore_wait(along_y, 3)
    for d in range(1, 4):
        pl.semaphore_signal(along_z, inc=1, device_id=place(x, y, z + d, c), device_id_type=MESH)
    for h in range(16):
        gathered[0, :, h * 128 : (h + 1) * 128] = attended[:, h, :].astype(bf16)
    pl.semaphore_wait(along_z, 3)

    for d in range(1, 8):
        to = (y * 8 + lax.rem(at + d, 8), kv)
        pltpu.make_async_remote_copy(
            src_ref=gathered.at[0], dst_ref=gathered.at[d], send_sem=a_send_sem.at[d - 1],
            recv_sem=a_recv_sem, device_id=to, device_id_type=MESH,
        ).start()

    routes_padded[...] = jnp.zeros((16, 8), jnp.int32)
    routes_padded[:12, :] = routes_ref[...]
    weights_padded[...] = jnp.zeros((16, 8), f32)
    weights_padded[:12, :] = weights_ref[...]
    state[...] = jnp.zeros((16, 4096), f32)
    state[:12, :] = residual_ref[...].astype(f32)
    partial[384:, :] = jnp.zeros((8, 512), f32)

    lane = iota((8, 128), 1)
    sub = iota((8, 128), 0)
    token = lane & 15
    expert = jnp.full((8, 128), -1, jnp.int32)
    for t in range(12):
        for k in range(8):
            expert = jnp.where((sub == k) & (token == t), routes_smem[t, k], expert)
    keys_row = route_keys(expert, token, routes_smem, me)
    for part in range(8):
        row = iota((256, 128), 0) + part * 256
        hit = jnp.zeros((256, 128), f32)
        for k in range(8):
            hit = jnp.where(row // 8 == keys_row[k : k + 1, :], 1.0, hit)
        hit = jnp.where((row & 7) == iota((256, 128), 1) // 16, hit, 0.0)
        table[part * 256 : (part + 1) * 256, :] = hit.astype(bf16)

    expert_column = jnp.concatenate([routes_padded[...]] * 8, axis=0)
    token_column = iota((128, 8), 0) & 15
    key_column = route_keys(expert_column, token_column, routes_smem, me)
    gates = jnp.concatenate([weights_padded[...]] * 8, axis=0)
    for part in range(8):
        column = iota((128, 256), 1) + part * 256
        share = jnp.zeros((128, 256), f32)
        for k in range(8):
            share = jnp.where(column // 8 == key_column[:, k : k + 1], gates[:, k : k + 1], share)
        share = jnp.where((column & 7) == iota((128, 256), 0) // 16, share, 0.0)
        high = share.astype(bf16)
        mix[:128, part * 256 : (part + 1) * 256] = high
        mix[128:, part * 256 : (part + 1) * 256] = (share - high.astype(f32)).astype(bf16)

    o_own.wait()
    landed = projection.at[:, pl.ds(128, 384)]
    pltpu.make_async_copy(landed, landed, o_recv_sem).wait()
    landed = gathered.at[pl.ds(1, 7)]
    pltpu.make_async_copy(landed, landed, a_recv_sem).wait()
    for n in range(2):
        columns = slice(n * 256, (n + 1) * 256)
        partial[:384, columns] = jnp.dot(
            gathered[...].reshape(384, 2048), projection[:, columns], preferred_element_type=f32
        )
    for d in range(8):
        for k in range(4):
            start = ((8 - d) % 8) * 48 + k * 12
            pieces[d, k] = partial[start : start + 16, :].astype(bf16)

    def hand_out(q, carry):
        d, e = q // 4, lax.rem(q, 4)
        to = lax.rem(kv + e, 4)
        pltpu.make_async_remote_copy(
            src_ref=pieces.at[d, to], dst_ref=collected.at[q], send_sem=p_send_sem, recv_sem=p_recv_sem,
            device_id=(y * 8 + lax.rem(at + d, 8), to), device_id_type=MESH,
        ).start()
        return carry

    lax.fori_loop(1, 32, hand_out, 0)
    collected[0] = pieces[0, kv]
    landed = collected.at[pl.ds(1, 31)]
    pltpu.make_async_copy(landed, landed, p_recv_sem).wait()
    square = jnp.zeros((16, 128), f32)
    for p in range(8):
        slot = lax.rem(at + 8 - p, 8) * 4
        for w in range(4):
            piece = pl.ds(pl.multiple_of(lax.rem(y + 4 - w, 4) * 128, 128), 128)
            total = collected[slot, :, piece].astype(f32)
            for e in range(1, 4):
                total = total + collected[slot + e, :, piece].astype(f32)
            columns = slice((w * 8 + p) * 128, (w * 8 + p + 1) * 128)
            total = state[:, columns] + total
            state[:, columns] = total
            square = square + total * total
    factor = lax.rsqrt(jnp.sum(square, axis=1, keepdims=True) * (1.0 / 4096.0) + 1e-06)
    for s in range(8):
        columns = slice(s * 512, (s + 1) * 512)
        normed[s * 16 : (s + 1) * 16, :] = (state[:, columns] * factor * gain_ref[:, columns]).astype(bf16)

    for part in range(8):
        block = jnp.dot(
            table[part * 256 : (part + 1) * 256, :], normed[...], preferred_element_type=f32
        ).astype(bf16)
        sent[part * 16 : (part + 1) * 16] = block.reshape(16, 16, 512)

    def send(d, carry):
        to = lax.rem(me + d * K_STEP, N_DEV)
        group = d // 64
        pltpu.make_async_remote_copy(
            src_ref=sent.at[d], dst_ref=received.at[d], send_sem=send_sem.at[group],
            recv_sem=recv_sem.at[group], device_id=(to // 4, lax.rem(to, 4)), device_id_type=MESH,
        ).start()
        return carry

    lax.fori_loop(1, N_DEV, send, 0)
    received[0] = sent[0]

    i, j = iota((256, 256), 0), iota((256, 256), 1)
    spread = jnp.where(j == (i & 31) * 8 + i // 32, 1.0, 0.0).astype(bf16)
    gather = jnp.where(i == (j & 31) * 8 + j // 32, 1.0, 0.0).astype(bf16)

    for group in range(2):
        first = 1 if group == 0 else 64
        landed = received.at[pl.ds(first, 64 * (group + 1) - first)]
        pltpu.make_async_copy(landed, landed, recv_sem.at[group]).wait()
        for chunk in range(4):
            block = received[group * 64 + chunk * 16 : group * 64 + (chunk + 1) * 16].reshape(256, 512)
            block = jnp.dot(spread, block, preferred_element_type=f32).astype(bf16)
            for s in range(8):
                rows[chunk * 32 : (chunk + 1) * 32, s * 512 : (s + 1) * 512] = block[s * 32 : (s + 1) * 32]
        if group == 0:
            loads[0].wait()
        for n in range(3):
            gate = jnp.dot(rows[...], gate_up[:, n * 256 : (n + 1) * 256], preferred_element_type=f32)
            up = jnp.dot(rows[...], gate_up[:, 768 + n * 256 : 768 + (n + 1) * 256], preferred_element_type=f32)
            active[:, n * 256 : (n + 1) * 256] = (gate / (1.0 + jnp.exp(-gate)) * up).astype(bf16)
        if group == 0:
            loads[1].wait()
        for s in range(8):
            part = jnp.dot(active[...], down[:, s * 512 : (s + 1) * 512], preferred_element_type=f32).astype(bf16)
            for chunk in range(4):
                permuted[chunk, s * 32 : (s + 1) * 32, :] = part[chunk * 32 : (chunk + 1) * 32]
        for chunk in range(4):
            block = jnp.dot(gather, permuted[chunk], preferred_element_type=f32).astype(bf16)
            results[group * 64 + chunk * 16 : group * 64 + (chunk + 1) * 16] = block.reshape(16, 16, 512)

        def send_back(d, carry):
            to = lax.rem(me + N_DEV * K_STEP - d * K_STEP, N_DEV)
            pltpu.make_async_remote_copy(
                src_ref=results.at[d], dst_ref=returned.at[d], send_sem=back_sem.at[0],
                recv_sem=return_sem.at[0], device_id=(to // 4, lax.rem(to, 4)), device_id_type=MESH,
            ).start()
            return carry

        lax.fori_loop(first, 64 * (group + 1), send_back, 0)
        if group == 0:
            returned[0] = results[0]

    landed = returned.at[pl.ds(1, 127)]
    pltpu.make_async_copy(landed, landed, return_sem.at[0]).wait()
    both = jnp.dot(mix[...], returned[...].reshape(2048, 512), preferred_element_type=f32)
    blended = both[:128] + both[128:]
    for s in range(8):
        columns = slice(s * 512, (s + 1) * 512)
        total = state[:, columns] + blended[s * 16 : (s + 1) * 16]
        out_ref[:, columns] = total[:12].astype(bf16)
    gone = sent.at[pl.ds(1, 63)]
    pltpu.make_async_copy(gone, gone, send_sem.at[0]).wait()
    gone = sent.at[pl.ds(64, 64)]
    pltpu.make_async_copy(gone, gone, send_sem.at[1]).wait()
    gone = results.at[pl.ds(1, 127)]
    pltpu.make_async_copy(gone, gone, back_sem.at[0]).wait()
    for d in range(1, 4):
        pltpu.make_async_copy(o_proj_hbm, projection.at[:, pl.ds(d * 128, 128)], o_send_sem.at[d - 1]).wait()
        pltpu.make_async_copy(gathered.at[0], gathered.at[d], a_send_sem.at[d - 1]).wait()
    for d in range(4, 8):
        pltpu.make_async_copy(gathered.at[0], gathered.at[d], a_send_sem.at[d - 1]).wait()
    gone = collected.at[pl.ds(1, 31)]
    pltpu.make_async_copy(gone, gone, p_send_sem).wait()


def body(
    queries, keys, values, lengths, o_proj, residual, norm_gain, gate_up, down, routes, route_weights,
):
    bf16, f32 = jnp.bfloat16, jnp.float32
    vmem = pl.BlockSpec(memory_space=pltpu.VMEM)
    smem = pl.BlockSpec(memory_space=pltpu.SMEM)
    hbm = pl.BlockSpec(memory_space=pl.ANY)
    dma, plain = pltpu.SemaphoreType.DMA, pltpu.SemaphoreType.REGULAR
    return pl.pallas_call(
        kernel,
        out_shape=jax.ShapeDtypeStruct((12, 4096), bf16),
        in_specs=[vmem, hbm, hbm, smem, hbm, vmem, vmem, smem, vmem, vmem, hbm, hbm],
        out_specs=vmem,
        scratch_shapes=[
            pltpu.VMEM((48, 192, 128), bf16),
            pltpu.VMEM((48, 192, 128), bf16),
            pltpu.VMEM((48, 16, 128), f32),
            pltpu.VMEM((48, 16, 128), f32),
            pltpu.VMEM((8, 48, 2048), bf16),
            pltpu.VMEM((2048, 512), bf16),
            pltpu.VMEM((392, 512), f32),
            pltpu.VMEM((8, 4, 16, 512), bf16),
            pltpu.VMEM((32, 16, 512), bf16),
            pltpu.VMEM((16, 4096), f32),
            pltpu.VMEM((16, 8), jnp.int32),
            pltpu.VMEM((16, 8), f32),
            pltpu.VMEM((4096, 1536), bf16),
            pltpu.VMEM((768, 4096), bf16),
            pltpu.VMEM((128, 16, 512), bf16),
            pltpu.VMEM((128, 16, 512), bf16),
            pltpu.VMEM((128, 4096), bf16),
            pltpu.VMEM((128, 768), bf16),
            pltpu.VMEM((4, 256, 512), bf16),
            pltpu.VMEM((128, 16, 512), bf16),
            pltpu.VMEM((128, 16, 512), bf16),
            pltpu.VMEM((128, 512), bf16),
            pltpu.VMEM((256, 2048), bf16),
            pltpu.VMEM((2048, 128), bf16),
            dma((2, 4)), dma((2,)), dma, dma((3,)), dma, dma((7,)), dma, dma, dma,
            dma((2,)), dma((2,)), dma((1,)), dma((1,)), plain, plain,
        ],
        compiler_params=pltpu.CompilerParams(
            collective_id=1, has_side_effects=True, vmem_limit_bytes=60 * 2**20
        ),
        cost_estimate=pl.CostEstimate(flops=6 * 10**9, bytes_accessed=3 * 10**7, transcendentals=10**6),
        name="layer",
    )(
        queries, keys[:, 0], values[:, 0], lengths, o_proj, residual, norm_gain[None, :], routes, routes,
        route_weights, gate_up[0], down[0],
    )


def solution(mesh):
    in_specs = (
        P("req", "kvh"),
        P("req", "kvh", None, None),
        P("req", "kvh", None, None),
        P("req"),
        P("kvh", "req"),
        P(("req", "kvh"), None),
        P(),
        P(("req", "kvh"), None, None),
        P(("req", "kvh"), None, None),
        P(("req", "kvh"), None),
        P(("req", "kvh"), None),
    )
    out_specs = P(("req", "kvh"), None)
    return jax.shard_map(body, mesh=mesh, in_specs=in_specs, out_specs=out_specs, check_vma=False)
```

time: 227 us -> 113 us (0.50)
  waiting for transfers between devices: 122 us -> 0 us
  Pallas kernels: 59 us -> 108 us
  between operations: 13.5 us -> 0.01 us
  matrix products: 9.9 us -> 0 us
  starting transfers between devices: 9.41 us -> 0 us
  local copies, waits for them, and re-layouts: 11.9 us -> 4.28 us
    all_gather x1 -> x0, waiting for transfers between devices: 94.8 us -> none  [body(): lax.all_gather(attended, 'req', axis=0, tiled=True)]
    pallas_call x1, Pallas kernels: 59 us -> 108 us  [body(): pl.pallas_call(kernel, out_shape=jax.ShapeDtypeStruct((12, 4096), bf16),...]
    reduce_scatter x1 -> x0, waiting for transfers between devices: 18.1 us -> none  [body(): summed = lax.psum_scatter(ordered, 'kvh', scatter_dimension=0, tiled=True)]
    dot_general x3 -> x0, matrix products: 9.9 us -> none  [the longest x1 5.53 us: body(): jnp.dot(lax.all_gather(attended, 'req', axis=0, tiled=True), o_proj, pref...]
    all_to_all x1 -> x0, starting transfers between devices: 9.37 us -> none  [body(): lax.all_to_all(summed, 'req', split_axis=0, concat_axis=1, tiled=True)]
    all_to_all x1 -> x0, waiting for transfers between devices: 8.9 us -> none  [body(): lax.all_to_all(summed, 'req', split_axis=0, concat_axis=1, tiled=True)]
    reshape x2 -> x0, local copies, waits for them, and re-layouts: 3.44 us -> none  [the longest x1 2.24 us: body(): ordered = partial_columns.reshape(req_count, group_count, tok_src, column...]
  transfers between devices with their start and end apart: 3 -> 0, of which waited for: 3 -> 0; matrix products, arithmetic and copies ran while one was open for 1% -> 0% of each run, Pallas kernels for 0% -> 0%
where the time goes in v2:
time: 113 us
  Pallas kernels  108 us (96%)
  local copies, waits for them, and re-layouts  4.28 us (4%)
    pallas_call x1, Pallas kernels, body(): pl.pallas_call(kernel, out_shape=jax.ShapeDtypeStruct((12, 4096), bf16),...  108 us
    unnamed x3, local copies, waits for them, and re-layouts  4.28 us

profile of v2, /device:TPU:1, one launch (start us, length us, event | category | flops | bytes accessed | tf_op | source)
XLA Modules:
  0.0 112.5 jit_solution(16493904539958825931)
XLA Ops:
  0.0 1.4 %copy.12.routes_smem.routes_ref = s32[12,8]{1,0:T(8,128)} copy(s32[12,8]{0,1:T(8,128)} %param.20) | data formatting | bytes 768 | tf_op args[9]
  1.4 1.4 %copy.14.weights_ref = f32[12,8]{1,0:T(8,128)} copy(f32[12,8]{0,1:T(8,128)} %param.21) | data formatting | bytes 768 | tf_op args[10]
  2.7 108.2 %layer.1 = bf16[12,4096]{1,0:T(8,128)(2,1)} custom-call(bf16[48,2048]{1,0:T(8,128)(2,1)} %queries_ref.1, bf16[48,192,128]{2,1,0:T(8,128)(2,1)} %bitcast.7, bf16[48,192,128]{2,1,0:T(8,128)(2,1)} %bitcast.8, s32[48]{0:T(128)} %lengths_smem.1, bf16[2048,128]{1,0:T(8,128)(2,1)} %o_proj_hbm.1, bf16[12,4096]{1,0:T(8,128)(2,1)} %residual_ref.1, f32[1,4096]{1,0:T(1,128)} %bitcast.9, ...), custom_call_target="tpu_custom_call" | custom-call | flops 6000000000 | bytes 30000000 | tf_op jit(solution)/shard_map/layer/pallas_call | solution.py:297
  110.9 1.6 %copy.16 = bf16[12,4096]{1,0:T(8,128)(2,1)} copy(bf16[12,4096]{1,0:T(8,128)(2,1)} %layer.1) | data formatting | bytes 196608

commit v3 on v2

--- a/solution.py
+++ b/solution.py
@@ -29,28 +29,18 @@
     return lax.broadcasted_iota(jnp.int32, shape, dim)
 
 
-def route_keys(expert, token, routes_smem, me):
-    slot = jnp.zeros_like(expert)
-    for t in range(12):
-        for k in range(8):
-            slot = slot + jnp.where((expert == routes_smem[t, k]) & (token > t), 1, 0)
-    key = (((expert - me + N_DEV) * K_INV) & (N_DEV - 1)) * 2 + slot
-    return jnp.where(token < 12, key, -1)
-
-
 def kernel(
-    queries_ref, keys_hbm, values_hbm, lengths_smem, o_proj_hbm, residual_ref, gain_ref, routes_smem, routes_ref,
-    weights_ref, gate_up_hbm, down_hbm,
+    queries_ref, keys_hbm, values_hbm, lengths_smem, o_proj_hbm, residual_ref, gain_ref, routes_smem, weights_smem,
+    gate_up_hbm, down_hbm,
     out_ref,
-    keys, values, heads, attended, gathered, projection, partial, pieces, collected, state, routes_padded,
-    weights_padded, gate_up, down, sent, received, rows, active, permuted, results, returned, normed, mix, table,
+    keys, values, heads, attended, gathered, projection, partial, staged, pieces, collected, summed, state, gate_up, down, sent, received, rows, active, permuted, results, returned, normed, mix, table,
     cache_sem, weight_sem, o_own_sem, o_send_sem, o_recv_sem, a_send_sem, a_recv_sem, p_send_sem, p_recv_sem,
     send_sem, recv_sem, back_sem, return_sem, along_y, along_z,
 ):
     r, kv = lax.axis_index("req"), lax.axis_index("kvh")
     me = r * 4 + kv
     x, y, z, c = coords()
-    at = lax.rem(r, 8)
+    half = lax.rem(r, 2)
     bf16, f32 = jnp.bfloat16, jnp.float32
 
     barrier = pltpu.get_barrier_semaphore()
@@ -62,14 +52,14 @@
         pl.semaphore_signal(barrier, inc=1, device_id=place(x, y + d, z, c), device_id_type=MESH)
         pl.semaphore_signal(barrier, inc=1, device_id=place(x, y, z + d, c), device_id_type=MESH)
 
-    def cache_load(g, which):
+    def cache_load(m, which):
         source, target = ((keys_hbm, keys), (values_hbm, values))[which]
-        part = pl.ds(g * 12, 12)
-        return pltpu.make_async_copy(source.at[part], target.at[part], cache_sem.at[which, g])
-
-    for g in range(4):
-        cache_load(g, 0).start()
-        cache_load(g, 1).start()
+        part = pl.ds(m * 16, 16)
+        return pltpu.make_async_copy(source.at[part], target.at[part], cache_sem.at[which, m])
+
+    for m in range(3):
+        cache_load(m, 0).start()
+        cache_load(m, 1).start()
     o_own = pltpu.make_async_copy(o_proj_hbm, projection.at[:, pl.ds(0, 128)], o_own_sem)
     o_own.start()
     loads = [
@@ -81,62 +71,118 @@
     for h in range(16):
         heads[:, h, :] = queries_ref[:, h * 128 : (h + 1) * 128].astype(f32)
 
+    def o_copy(source, slot, part, n, dy, rows):
+        return pltpu.make_async_remote_copy(
+            src_ref=source, dst_ref=projection.at[pl.ds(part * 1024, rows), pl.ds(slot * 128, 128)],
+            send_sem=o_send_sem.at[n], recv_sem=o_recv_sem.at[n], device_id=place(x, y + dy, z, c),
+            device_id_type=MESH,
+        )
+
+    def o_first(n):
+        slot, part, dy = ((1, 0, 1), (3, 1, 3), (1, 1, 1), (3, 0, 3))[n]
+        return o_copy(o_proj_hbm.at[pl.ds(part * 1024, 1024)], slot, part, n, dy, 1024)
+
+    def o_pass(n):
+        slot, part, dy = ((1, 0, 1), (3, 1, 3))[n]
+        held = projection.at[pl.ds(part * 1024, 1024), pl.ds(slot * 128, 128)]
+        return o_copy(held, 2, part, 4 + n, dy, 1024)
+
     pl.semaphore_wait(barrier, 13)
-    for d in range(1, 4):
-        pltpu.make_async_remote_copy(
-            src_ref=o_proj_hbm, dst_ref=projection.at[:, pl.ds(d * 128, 128)], send_sem=o_send_sem.at[d - 1],
-            recv_sem=o_recv_sem, device_id=place(x, y + d, z, c), device_id_type=MESH,
-        ).start()
+    for n in range(4):
+        o_first(n).start()
     for d in range(1, 4):
         pl.semaphore_signal(along_y, inc=1, device_id=place(x, y + d, z, c), device_id_type=MESH)
 
-    position = iota((16, 192), 1)
-
-    def attend(g, carry):
-        cache_load(g, 0).wait()
-        cache_load(g, 1).wait()
-        for b in range(12):
-            i = g * 12 + b
-            scores = lax.dot_general(
-                heads[i].astype(bf16), keys[i], (((1,), (1,)), ((), ())), preferred_element_type=f32
-            ) * (1.0 / math.sqrt(128.0))
-            scores = jnp.where(position < lengths_smem[i], scores, -1e30)
-            shifted = jnp.exp(scores - jnp.max(scores, axis=1, keepdims=True))
-            shares = (shifted / jnp.sum(shifted, axis=1, keepdims=True)).astype(bf16)
-            attended[i] = jnp.dot(shares, values[i], preferred_element_type=f32)
-        return carry
-
-    lax.fori_loop(0, 4, attend, 0)
-    pl.semaphore_wait(along_y, 3)
-    for d in range(1, 4):
-        pl.semaphore_signal(along_z, inc=1, device_id=place(x, y, z + d, c), device_id_type=MESH)
-    for h in range(16):
-        gathered[0, :, h * 128 : (h + 1) * 128] = attended[:, h, :].astype(bf16)
-    pl.semaphore_wait(along_z, 3)
-
-    for d in range(1, 8):
-        to = (y * 8 + lax.rem(at + d, 8), kv)
-        pltpu.make_async_remote_copy(
-            src_ref=gathered.at[0], dst_ref=gathered.at[d], send_sem=a_send_sem.at[d - 1],
-            recv_sem=a_recv_sem, device_id=to, device_id_type=MESH,
-        ).start()
-
-    routes_padded[...] = jnp.zeros((16, 8), jnp.int32)
-    routes_padded[:12, :] = routes_ref[...]
-    weights_padded[...] = jnp.zeros((16, 8), f32)
-    weights_padded[:12, :] = weights_ref[...]
+    position = iota((192, 128), 0)
+    request = iota((128, 128), 1) // 16
+
+    def attend(g):
+        first = g * 8
+        turned = jnp.transpose(heads[first : first + 8].reshape(128, 128))
+        scores = jnp.zeros((192, 128), f32)
+        for b in range(0, 8, 2):
+            two = jnp.concatenate([keys[first + b], keys[first + b + 1]], axis=1)
+            asked = jnp.concatenate(
+                [jnp.where(request == b, turned, 0.0), jnp.where(request == b + 1, turned, 0.0)], axis=0
+            ).astype(bf16)
+            scores = scores + jnp.dot(two, asked, preferred_element_type=f32)
+        scores = scores * (1.0 / math.sqrt(128.0))
+        limit = jnp.zeros((1, 128), jnp.int32)
+        for b in range(8):
+            limit = jnp.where(request[:1] == b, lengths_smem[first + b], limit)
+        scores = jnp.where(position < limit, scores, -1e30)
+        shifted = jnp.exp(scores - jnp.max(scores, axis=0, keepdims=True))
+        shares = shifted / jnp.sum(shifted, axis=0, keepdims=True)
+        shares = jnp.transpose(shares).astype(bf16)
+        for b in range(8):
+            attended[first + b] = jnp.dot(
+                shares[b * 16 : (b + 1) * 16], values[first + b], preferred_element_type=f32
+            )
+
+    def a_copy(slot, m, dz, dh):
+        part = pl.ds(m * 16, 16)
+        to = ((y * 4 + lax.rem(z + dz, 4)) * 2 + lax.rem(half + dh, 2), kv)
+        return pltpu.make_async_remote_copy(
+            src_ref=gathered.at[slot, part], dst_ref=gathered.at[slot + dz * 2 + dh, part], send_sem=a_send_sem,
+            recv_sem=a_recv_sem.at[m, slot + dz * 2 + dh], device_id=to, device_id_type=MESH,
+        )
+
+    def a_wait(m, slot):
+        landed = gathered.at[slot, pl.ds(m * 16, 16)]
+        pltpu.make_async_copy(landed, landed, a_recv_sem.at[m, slot]).wait()
+
+    def a_start(m):
+        rows_here = slice(m * 16, (m + 1) * 16)
+        for h in range(16):
+            gathered[0, rows_here, h * 128 : (h + 1) * 128] = attended[rows_here, h, :].astype(bf16)
+
+    def a_send(m):
+        a_copy(0, m, 0, 1).start()
+        for dz in (1, 3, 2):
+            a_copy(0, m, dz, 0).start()
+
+    for m in range(3):
+        cache_load(m, 0).wait()
+        cache_load(m, 1).wait()
+        attend(2 * m)
+        attend(2 * m + 1)
+        a_start(m)
+        if m == 0:
+            pl.semaphore_wait(along_y, 3)
+            for d in range(1, 4):
+                pl.semaphore_signal(along_z, inc=1, device_id=place(x, y, z + d, c), device_id_type=MESH)
+            pl.semaphore_wait(along_z, 3)
+        a_send(m)
+    for n in range(2):
+        pltpu.make_async_copy(o_proj_hbm.at[pl.ds(0, 1024)], projection.at[pl.ds(0, 1024), pl.ds(128, 128)], o_recv_sem.at[n]).wait()
+        o_pass(n).start()
+    a_wait(0, 1)
+    for dz in (1, 3, 2):
+        a_copy(1, 0, dz, 0).start()
+    for m in (1, 2):
+        for dz in (1, 3, 2):
+            a_wait(m, dz * 2)
+            a_copy(dz * 2, m, 0, 1).start()
+
     state[...] = jnp.zeros((16, 4096), f32)
     state[:12, :] = residual_ref[...].astype(f32)
-    partial[384:, :] = jnp.zeros((8, 512), f32)
 
     lane = iota((8, 128), 1)
     sub = iota((8, 128), 0)
     token = lane & 15
     expert = jnp.full((8, 128), -1, jnp.int32)
+    gates = jnp.zeros((8, 128), f32)
     for t in range(12):
         for k in range(8):
-            expert = jnp.where((sub == k) & (token == t), routes_smem[t, k], expert)
-    keys_row = route_keys(expert, token, routes_smem, me)
+            here = (sub == k) & (token == t)
+            expert = jnp.where(here, routes_smem[k, t], expert)
+            gates = jnp.where(here, weights_smem[k, t], gates)
+    slot_of = jnp.zeros((8, 128), jnp.int32)
+    for t in range(12):
+        for k in range(8):
+            slot_of = slot_of + jnp.where((expert == routes_smem[k, t]) & (token > t), 1, 0)
+    keys_row = (((expert - me + N_DEV) * K_INV) & (N_DEV - 1)) * 2 + slot_of
+    keys_row = jnp.where(token < 12, keys_row, -1)
     for part in range(8):
         row = iota((256, 128), 0) + part * 256
         hit = jnp.zeros((256, 128), f32)
@@ -145,10 +191,8 @@
         hit = jnp.where((row & 7) == iota((256, 128), 1) // 16, hit, 0.0)
         table[part * 256 : (part + 1) * 256, :] = hit.astype(bf16)
 
-    expert_column = jnp.concatenate([routes_padded[...]] * 8, axis=0)
-    token_column = iota((128, 8), 0) & 15
-    key_column = route_keys(expert_column, token_column, routes_smem, me)
-    gates = jnp.concatenate([weights_padded[...]] * 8, axis=0)
+    key_column = jnp.transpose(keys_row.astype(f32)).astype(jnp.int32)
+    gates = jnp.transpose(gates)
     for part in range(8):
         column = iota((128, 256), 1) + part * 256
         share = jnp.zeros((128, 256), f32)
@@ -160,49 +204,57 @@
         mix[128:, part * 256 : (part + 1) * 256] = (share - high.astype(f32)).astype(bf16)
 
     o_own.wait()
-    landed = projection.at[:, pl.ds(128, 384)]
-    pltpu.make_async_copy(landed, landed, o_recv_sem).wait()
-    landed = gathered.at[pl.ds(1, 7)]
-    pltpu.make_async_copy(landed, landed, a_recv_sem).wait()
+    for n in range(2, 6):
+        pltpu.make_async_copy(o_proj_hbm.at[pl.ds(0, 1024)], projection.at[pl.ds(0, 1024), pl.ds(128, 128)], o_recv_sem.at[n]).wait()
+    for m in range(3):
+        for slot in range(1, 8):
+            if not (slot == 1 and m == 0 or slot in (2, 4, 6) and m > 0):
+                a_wait(m, slot)
     for n in range(2):
         columns = slice(n * 256, (n + 1) * 256)
-        partial[:384, columns] = jnp.dot(
+        partial[:, columns] = jnp.dot(
             gathered[...].reshape(384, 2048), projection[:, columns], preferred_element_type=f32
         )
     for d in range(8):
+        slot = ((4 - d // 2) % 4) * 2 + d % 2
         for k in range(4):
-            start = ((8 - d) % 8) * 48 + k * 12
-            pieces[d, k] = partial[start : start + 16, :].astype(bf16)
+            for w in range(4):
+                staged[d * 4 + k, w * 12 : (w + 1) * 12, :] = partial[
+                    slot * 48 + k * 12 : slot * 48 + (k + 1) * 12, w * 128 : (w + 1) * 128
+                ]
+        pieces[d * 4 : d * 4 + 4] = staged[d * 4 : d * 4 + 4].astype(bf16)
 
     def hand_out(q, carry):
         d, e = q // 4, lax.rem(q, 4)
         to = lax.rem(kv + e, 4)
+        there = (y * 4 + lax.rem(z + d // 2, 4)) * 2 + lax.rem(half + lax.rem(d, 2), 2)
         pltpu.make_async_remote_copy(
-            src_ref=pieces.at[d, to], dst_ref=collected.at[q], send_sem=p_send_sem, recv_sem=p_recv_sem,
-            device_id=(y * 8 + lax.rem(at + d, 8), to), device_id_type=MESH,
+            src_ref=pieces.at[d * 4 + to], dst_ref=collected.at[q], send_sem=p_send_sem, recv_sem=p_recv_sem,
+            device_id=(there, to), device_id_type=MESH,
         ).start()
         return carry
 
     lax.fori_loop(1, 32, hand_out, 0)
-    collected[0] = pieces[0, kv]
+    collected[0] = pieces[kv]
     landed = collected.at[pl.ds(1, 31)]
     pltpu.make_async_copy(landed, landed, p_recv_sem).wait()
-    square = jnp.zeros((16, 128), f32)
+    square = jnp.zeros((12, 128), f32)
     for p in range(8):
-        slot = lax.rem(at + 8 - p, 8) * 4
+        slot = (lax.rem(z + 4 - p // 2, 4) * 2 + lax.rem(half + p % 2, 2)) * 4
+        total = collected[slot].astype(f32)
+        for e in range(1, 4):
+            total = total + collected[slot + e].astype(f32)
+        summed[p] = total
         for w in range(4):
-            piece = pl.ds(pl.multiple_of(lax.rem(y + 4 - w, 4) * 128, 128), 128)
-            total = collected[slot, :, piece].astype(f32)
-            for e in range(1, 4):
-                total = total + collected[slot + e, :, piece].astype(f32)
-            columns = slice((w * 8 + p) * 128, (w * 8 + p + 1) * 128)
-            total = state[:, columns] + total
-            state[:, columns] = total
+            columns = pl.ds(pl.multiple_of((lax.rem(y + 4 - w, 4) * 8 + p) * 128, 128), 128)
+            total = state[:12, columns] + summed[p, w * 12 : (w + 1) * 12, :]
+            state[:12, columns] = total
             square = square + total * total
     factor = lax.rsqrt(jnp.sum(square, axis=1, keepdims=True) * (1.0 / 4096.0) + 1e-06)
+    normed[...] = jnp.zeros((128, 512), bf16)
     for s in range(8):
         columns = slice(s * 512, (s + 1) * 512)
-        normed[s * 16 : (s + 1) * 16, :] = (state[:, columns] * factor * gain_ref[:, columns]).astype(bf16)
+        normed[s * 16 : s * 16 + 12, :] = (state[:12, columns] * factor * gain_ref[:, columns]).astype(bf16)
 
     for part in range(8):
         block = jnp.dot(
@@ -277,11 +329,10 @@
     pltpu.make_async_copy(gone, gone, send_sem.at[1]).wait()
     gone = results.at[pl.ds(1, 127)]
     pltpu.make_async_copy(gone, gone, back_sem.at[0]).wait()
-    for d in range(1, 4):
-        pltpu.make_async_copy(o_proj_hbm, projection.at[:, pl.ds(d * 128, 128)], o_send_sem.at[d - 1]).wait()
-        pltpu.make_async_copy(gathered.at[0], gathered.at[d], a_send_sem.at[d - 1]).wait()
-    for d in range(4, 8):
-        pltpu.make_async_copy(gathered.at[0], gathered.at[d], a_send_sem.at[d - 1]).wait()
+    for n in range(6):
+        pltpu.make_async_copy(o_proj_hbm.at[pl.ds(0, 1024)], projection.at[pl.ds(0, 1024), pl.ds(128, 128)], o_send_sem.at[n]).wait()
+    gone = gathered.at[pl.ds(1, 7)]
+    pltpu.make_async_copy(gone, gone, a_send_sem).wait()
     gone = collected.at[pl.ds(1, 31)]
     pltpu.make_async_copy(gone, gone, p_send_sem).wait()
 
@@ -297,7 +348,7 @@
     return pl.pallas_call(
         kernel,
         out_shape=jax.ShapeDtypeStruct((12, 4096), bf16),
-        in_specs=[vmem, hbm, hbm, smem, hbm, vmem, vmem, smem, vmem, vmem, hbm, hbm],
+        in_specs=[vmem, hbm, hbm, smem, hbm, vmem, vmem, smem, smem, hbm, hbm],
         out_specs=vmem,
         scratch_shapes=[
             pltpu.VMEM((48, 192, 128), bf16),
@@ -306,12 +357,12 @@
             pltpu.VMEM((48, 16, 128), f32),
             pltpu.VMEM((8, 48, 2048), bf16),
             pltpu.VMEM((2048, 512), bf16),
-            pltpu.VMEM((392, 512), f32),
-            pltpu.VMEM((8, 4, 16, 512), bf16),
-            pltpu.VMEM((32, 16, 512), bf16),
+            pltpu.VMEM((384, 512), f32),
+            pltpu.VMEM((32, 48, 128), f32),
+            pltpu.VMEM((32, 48, 128), bf16),
+            pltpu.VMEM((32, 48, 128), bf16),
+            pltpu.VMEM((8, 48, 128), f32),
             pltpu.VMEM((16, 4096), f32),
-            pltpu.VMEM((16, 8), jnp.int32),
-            pltpu.VMEM((16, 8), f32),
             pltpu.VMEM((4096, 1536), bf16),
             pltpu.VMEM((768, 4096), bf16),
             pltpu.VMEM((128, 16, 512), bf16),
@@ -324,7 +375,7 @@
             pltpu.VMEM((128, 512), bf16),
             pltpu.VMEM((256, 2048), bf16),
             pltpu.VMEM((2048, 128), bf16),
-            dma((2, 4)), dma((2,)), dma, dma((3,)), dma, dma((7,)), dma, dma, dma,
+            dma((2, 3)), dma((2,)), dma, dma((6,)), dma((6,)), dma, dma((3, 8)), dma, dma,
             dma((2,)), dma((2,)), dma((1,)), dma((1,)), plain, plain,
         ],
         compiler_params=pltpu.CompilerParams(
@@ -333,8 +384,8 @@
         cost_estimate=pl.CostEstimate(flops=6 * 10**9, bytes_accessed=3 * 10**7, transcendentals=10**6),
         name="layer",
     )(
-        queries, keys[:, 0], values[:, 0], lengths, o_proj, residual, norm_gain[None, :], routes, routes,
-        route_weights, gate_up[0], down[0],
+        queries, keys[:, 0], values[:, 0], lengths, o_proj, residual, norm_gain[None, :], routes.T,
+        route_weights.T, gate_up[0], down[0],
     )
 
 

time: 113 us -> 90.5 us (0.80)
  Pallas kernels: 108 us -> 88.8 us
  local copies, waits for them, and re-layouts: 4.28 us -> 1.57 us
    pallas_call x1, Pallas kernels: 108 us -> 88.8 us  [body(): pl.pallas_call(kernel, out_shape=jax.ShapeDtypeStruct((12, 4096), bf16),...]
    unnamed x3 -> x1, local copies, waits for them, and re-layouts: 4.28 us -> 1.57 us
where the time goes in v3:
time: 90.5 us; the launch traced here: 90.4 us
  Pallas kernels  88.8 us (98%)
  local copies, waits for them, and re-layouts  1.57 us (2%)
    pallas_call x1, Pallas kernels, body(): pl.pallas_call(kernel, out_shape=jax.ShapeDtypeStruct((12, 4096), bf16),...  88.8 us

profile of v3, /device:TPU:1, one launch (start us, length us, event | category | flops | bytes accessed | tf_op | source)
XLA Modules:
  0.0 90.4 jit_solution(13343424020056525072)
XLA Ops:
  0.0 88.8 %layer.1 = bf16[12,4096]{1,0:T(8,128)(2,1)} custom-call(bf16[48,2048]{1,0:T(8,128)(2,1)} %queries_ref.1, bf16[48,192,128]{2,1,0:T(8,128)(2,1)} %bitcast.9, bf16[48,192,128]{2,1,0:T(8,128)(2,1)} %bitcast.10, s32[48]{0:T(128)} %lengths_smem.1, bf16[2048,128]{1,0:T(8,128)(2,1)} %o_proj_hbm.1, bf16[12,4096]{1,0:T(8,128)(2,1)} %residual_ref.1, ...), custom_call_target="tpu_custom_call" | custom-call | flops 6000000000 | bytes 30000000 | tf_op jit(solution)/shard_map/layer/pallas_call | solution.py:348
  88.8 1.6 %copy.13 = bf16[12,4096]{1,0:T(8,128)(2,1)} copy(bf16[12,4096]{1,0:T(8,128)(2,1)} %layer.1) | data formatting | bytes 196608

commit v4 on v3

--- a/solution.py
+++ b/solution.py
@@ -8,9 +8,6 @@
 from jax.sharding import PartitionSpec as P
 
 
-K_STEP = 37
-K_INV = 45
-N_DEV = 128
 MESH = pl.DeviceIdType.MESH
 
 
@@ -29,19 +26,35 @@
     return lax.broadcasted_iota(jnp.int32, shape, dim)
 
 
+WIDTHS = (1536, 1280, 1280)
+STARTS = (0, 1536, 2816)
+
+
+def ahead(axis, d):
+    x, y, z, c = coords()
+    return ((x, y, z + d, c), (x, y + d, z, c), (x + d, y, z, c))[axis]
+
+
 def kernel(
     queries_ref, keys_hbm, values_hbm, lengths_smem, o_proj_hbm, residual_ref, gain_ref, routes_smem, weights_smem,
     gate_up_hbm, down_hbm,
     out_ref,
-    keys, values, heads, attended, gathered, projection, partial, staged, pieces, collected, summed, state, gate_up, down, sent, received, rows, active, permuted, results, returned, normed, mix, table,
+    keys, values, heads, attended, gathered, projection, partial, staged, pieces, collected, summed, state, gate_up,
+    down, tiles, line, sent, received, rows, active, results, returned, shared, arrived, table, mix, spread, gather,
     cache_sem, weight_sem, o_own_sem, o_send_sem, o_recv_sem, a_send_sem, a_recv_sem, p_send_sem, p_recv_sem,
-    send_sem, recv_sem, back_sem, return_sem, along_y, along_z,
+    tile_send_sem, tile_recv_sem, line_send_sem, line_recv_sem, send_sem, recv_sem, back_sem, return_sem,
+    share_send_sem, share_recv_sem, along_y, along_z,
 ):
     r, kv = lax.axis_index("req"), lax.axis_index("kvh")
-    me = r * 4 + kv
     x, y, z, c = coords()
     half = lax.rem(r, 2)
     bf16, f32 = jnp.bfloat16, jnp.float32
+
+    xs, ys, zs = ([lax.rem(at + d, 4) for d in range(4)] for at in (x, y, z))
+    high_x, low_x, cores = [at // 2 for at in xs], [lax.rem(at, 2) * 2 for at in xs], [c, 1 - c]
+
+    def away(dx, dy, dz, dc):
+        return ((ys[dy % 4] * 4 + zs[dz % 4]) * 2 + high_x[dx % 4], low_x[dx % 4] + cores[dc])
 
     barrier = pltpu.get_barrier_semaphore()
     for dx in range(4):
@@ -177,31 +190,68 @@
             here = (sub == k) & (token == t)
             expert = jnp.where(here, routes_smem[k, t], expert)
             gates = jnp.where(here, weights_smem[k, t], gates)
-    slot_of = jnp.zeros((8, 128), jnp.int32)
+    place_of = jnp.zeros((8, 128), jnp.int32)
     for t in range(12):
         for k in range(8):
-            slot_of = slot_of + jnp.where((expert == routes_smem[k, t]) & (token > t), 1, 0)
-    keys_row = (((expert - me + N_DEV) * K_INV) & (N_DEV - 1)) * 2 + slot_of
-    keys_row = jnp.where(token < 12, keys_row, -1)
-    for part in range(8):
-        row = iota((256, 128), 0) + part * 256
-        hit = jnp.zeros((256, 128), f32)
+            place_of = place_of + jnp.where((expert == routes_smem[k, t]) & (token > t), 1, 0)
+    tiles[9, :8, :] = jnp.where(token < 12, expert * 2 + place_of, -1).astype(f32)
+    tiles[9, 8:, :] = gates
+
+    for f in range(3):
+        for d in range(1, 4):
+            pltpu.make_async_remote_copy(
+                src_ref=tiles.at[9], dst_ref=tiles.at[f * 3 + d - 1], send_sem=tile_send_sem, recv_sem=tile_recv_sem,
+                device_id=place(*ahead(f, d)), device_id_type=MESH,
+            ).start()
+        line[f][0] = jnp.zeros((16, WIDTHS[f]), bf16)
+
+    for f in range(3):
+        def column(i):
+            half_of, n = i // 128, i & 127
+            dx, dy, dz, row = n // 32, (n // 8) & 3, (n // 2) & 3, n & 1
+            p, q, g = ((dx, dy, dz), (dx, dz, dy), (dy, dz, dx))[f]
+            return (p * 4 + q) * 16 + half_of * 8 + g * 2 + row
+
+        i, j = iota((256, 256), 0), iota((256, 256), 1)
+        spread[f] = jnp.where(j == column(i), 1.0, 0.0).astype(bf16)
+        gather[f] = jnp.where(i == column(j), 1.0, 0.0).astype(bf16)
+
+    landed = tiles.at[pl.ds(0, 9)]
+    pltpu.make_async_copy(landed, landed, tile_recv_sem).wait()
+    for f in range(3):
+        marks = jnp.full((8, 128), -1, jnp.int32)
+        gates = jnp.zeros((8, 128), f32)
+        for d in range(4):
+            tile = tiles[9] if d == 0 else tiles[f * 3 + d - 1]
+            marks = jnp.where(lane // 16 == d, tile[:8].astype(jnp.int32), marks)
+            gates = jnp.where(lane // 16 == d, tile[8:], gates)
+        number = marks // 2
+        ring, group = number // 4, number & 3
+        dx = ((ring & 1) * 2 + group // 2 + 4 - x) & 3
+        dy = (ring // 8 + 4 - y) & 3
+        dz = ((ring // 2) & 3) + 4 - z & 3
+        dc = ((group & 1) + 2 - c) & 1
+        p, q, g = ((dx, dy, dz), (dx, dz, dy), (dy, dz, dx))[f]
+        key = ((dc * 16 + p * 4 + q) * 4 + lane // 16) * 2 + (marks & 1)
+        key = jnp.where((marks >= 0) & (g == 0), key, -1)
+        row = iota((256, 64), 0)
+        hit = jnp.zeros((256, 64), f32)
         for k in range(8):
-            hit = jnp.where(row // 8 == keys_row[k : k + 1, :], 1.0, hit)
-        hit = jnp.where((row & 7) == iota((256, 128), 1) // 16, hit, 0.0)
-        table[part * 256 : (part + 1) * 256, :] = hit.astype(bf16)
-
-    key_column = jnp.transpose(keys_row.astype(f32)).astype(jnp.int32)
-    gates = jnp.transpose(gates)
-    for part in range(8):
-        column = iota((128, 256), 1) + part * 256
-        share = jnp.zeros((128, 256), f32)
+            hit = jnp.where(row == key[k : k + 1, :64], 1.0, hit)
+        table[f] = hit.astype(bf16)
+        key_column = jnp.transpose(key.astype(f32))[:64].astype(jnp.int32)
+        gate_column = jnp.transpose(gates)[:64]
+        spot = iota((64, 512), 1)
+        share = jnp.zeros((64, 512), f32)
         for k in range(8):
-            share = jnp.where(column // 8 == key_column[:, k : k + 1], gates[:, k : k + 1], share)
-        share = jnp.where((column & 7) == iota((128, 256), 0) // 16, share, 0.0)
-        high = share.astype(bf16)
-        mix[:128, part * 256 : (part + 1) * 256] = high
-        mix[128:, part * 256 : (part + 1) * 256] = (share - high.astype(f32)).astype(bf16)
+            share = jnp.where(
+                (spot // 16) * 8 + (spot & 7) == key_column[:, k : k + 1], gate_column[:, k : k + 1], share
+            )
+        for h in range(2):
+            part = jnp.where((spot // 8) & 1 == h, share, 0.0)
+            high = part.astype(bf16)
+            mix[f, h, :64, :] = high
+            mix[f, h, 64:, :] = (part - high.astype(f32)).astype(bf16)
 
     o_own.wait()
     for n in range(2, 6):
@@ -210,20 +260,6 @@
         for slot in range(1, 8):
             if not (slot == 1 and m == 0 or slot in (2, 4, 6) and m > 0):
                 a_wait(m, slot)
-    for n in range(2):
-        columns = slice(n * 256, (n + 1) * 256)
-        partial[:, columns] = jnp.dot(
-            gathered[...].reshape(384, 2048), projection[:, columns], preferred_element_type=f32
-        )
-    for d in range(8):
-        slot = ((4 - d // 2) % 4) * 2 + d % 2
-        for k in range(4):
-            for w in range(4):
-                staged[d * 4 + k, w * 12 : (w + 1) * 12, :] = partial[
-                    slot * 48 + k * 12 : slot * 48 + (k + 1) * 12, w * 128 : (w + 1) * 128
-                ]
-        pieces[d * 4 : d * 4 + 4] = staged[d * 4 : d * 4 + 4].astype(bf16)
-
     def hand_out(q, carry):
         d, e = q // 4, lax.rem(q, 4)
         to = lax.rem(kv + e, 4)
@@ -234,7 +270,20 @@
         ).start()
         return carry
 
-    lax.fori_loop(1, 32, hand_out, 0)
+    for turn in range(2):
+        slots = slice(turn * 4, turn * 4 + 4)
+        partial[turn * 192 : (turn + 1) * 192, :] = jnp.dot(
+            gathered[slots].reshape(192, 2048), projection[...], preferred_element_type=f32
+        )
+        for slot in range(turn * 4, turn * 4 + 4):
+            d = ((4 - slot // 2) % 4) * 2 + slot % 2
+            for k in range(4):
+                for w in range(4):
+                    staged[d * 4 + k, w * 12 : (w + 1) * 12, :] = partial[
+                        slot * 48 + k * 12 : slot * 48 + (k + 1) * 12, w * 128 : (w + 1) * 128
+                    ]
+            pieces[d * 4 : d * 4 + 4] = staged[d * 4 : d * 4 + 4].astype(bf16)
+            lax.fori_loop(d * 4 + (d == 0), d * 4 + 4, hand_out, 0)
     collected[0] = pieces[kv]
     landed = collected.at[pl.ds(1, 31)]
     pltpu.make_async_copy(landed, landed, p_recv_sem).wait()
@@ -251,42 +300,52 @@
             state[:12, columns] = total
             square = square + total * total
     factor = lax.rsqrt(jnp.sum(square, axis=1, keepdims=True) * (1.0 / 4096.0) + 1e-06)
-    normed[...] = jnp.zeros((128, 512), bf16)
-    for s in range(8):
-        columns = slice(s * 512, (s + 1) * 512)
-        normed[s * 16 : s * 16 + 12, :] = (state[:12, columns] * factor * gain_ref[:, columns]).astype(bf16)
-
-    for part in range(8):
-        block = jnp.dot(
-            table[part * 256 : (part + 1) * 256, :], normed[...], preferred_element_type=f32
-        ).astype(bf16)
-        sent[part * 16 : (part + 1) * 16] = block.reshape(16, 16, 512)
-
-    def send(d, carry):
-        to = lax.rem(me + d * K_STEP, N_DEV)
-        group = d // 64
-        pltpu.make_async_remote_copy(
-            src_ref=sent.at[d], dst_ref=received.at[d], send_sem=send_sem.at[group],
-            recv_sem=recv_sem.at[group], device_id=(to // 4, lax.rem(to, 4)), device_id_type=MESH,
-        ).start()
-        return carry
-
-    lax.fori_loop(1, N_DEV, send, 0)
-    received[0] = sent[0]
-
-    i, j = iota((256, 256), 0), iota((256, 256), 1)
-    spread = jnp.where(j == (i & 31) * 8 + i // 32, 1.0, 0.0).astype(bf16)
-    gather = jnp.where(i == (j & 31) * 8 + j // 32, 1.0, 0.0).astype(bf16)
+    for f in range(3):
+        columns = slice(STARTS[f], STARTS[f] + WIDTHS[f])
+        line[f][0, :12, :] = (state[:12, columns] * factor * gain_ref[:, columns]).astype(bf16)
+        for d in (2, 1, 3):
+            pltpu.make_async_remote_copy(
+                src_ref=line[f].at[0], dst_ref=line[f].at[d], send_sem=line_send_sem.at[f],
+                recv_sem=line_recv_sem.at[f], device_id=place(*ahead(f, d)), device_id_type=MESH,
+            ).start()
+
+    def across(f, j, sign):
+        p, q, dc = sign * (j // 4 % 4), sign * (j % 4), j // 16
+        return away(*((p, q, 0, dc), (p, 0, q, dc), (0, p, q, dc))[f])
 
     for group in range(2):
-        first = 1 if group == 0 else 64
-        landed = received.at[pl.ds(first, 64 * (group + 1) - first)]
-        pltpu.make_async_copy(landed, landed, recv_sem.at[group]).wait()
-        for chunk in range(4):
-            block = received[group * 64 + chunk * 16 : group * 64 + (chunk + 1) * 16].reshape(256, 512)
-            block = jnp.dot(spread, block, preferred_element_type=f32).astype(bf16)
-            for s in range(8):
-                rows[chunk * 32 : (chunk + 1) * 32, s * 512 : (s + 1) * 512] = block[s * 32 : (s + 1) * 32]
+        blocks = range(group * 16, group * 16 + 16)
+        for f in range(3):
+            width = WIDTHS[f] // 2
+            if group == 0:
+                landed = line[f].at[pl.ds(1, 3)]
+                pltpu.make_async_copy(landed, landed, line_recv_sem.at[f]).wait()
+            block = jnp.dot(
+                table[f, group * 128 : (group + 1) * 128], line[f][...].reshape(64, WIDTHS[f]),
+                preferred_element_type=f32,
+            ).reshape(16, 8, WIDTHS[f])
+            sent[f][group * 16 : (group + 1) * 16] = jnp.concatenate(
+                [block[:, :, :width], block[:, :, width:]], axis=1
+            ).astype(bf16)
+            for j in blocks:
+                if j:
+                    pltpu.make_async_remote_copy(
+                        src_ref=sent[f].at[j], dst_ref=received[f].at[j], send_sem=send_sem.at[f],
+                        recv_sem=recv_sem.at[f, group], device_id=across(f, j, 1), device_id_type=MESH,
+                    ).start()
+    for f in range(3):
+        received[f][0] = sent[f][0]
+
+    for group in range(2):
+        first = 1 - group
+        for f in range(3):
+            width, start = WIDTHS[f] // 2, STARTS[f]
+            landed = received[f].at[pl.ds(group * 16 + first, 16 - first)]
+            pltpu.make_async_copy(landed, landed, recv_sem.at[f, group]).wait()
+            block = received[f][group * 16 : (group + 1) * 16].reshape(256, width)
+            block = jnp.dot(spread[f], block, preferred_element_type=f32).astype(bf16)
+            for h in range(2):
+                rows[:, start + h * width : start + (h + 1) * width] = block[h * 128 : (h + 1) * 128]
         if group == 0:
             loads[0].wait()
         for n in range(3):
@@ -295,46 +354,63 @@
             active[:, n * 256 : (n + 1) * 256] = (gate / (1.0 + jnp.exp(-gate)) * up).astype(bf16)
         if group == 0:
             loads[1].wait()
-        for s in range(8):
-            part = jnp.dot(active[...], down[:, s * 512 : (s + 1) * 512], preferred_element_type=f32).astype(bf16)
-            for chunk in range(4):
-                permuted[chunk, s * 32 : (s + 1) * 32, :] = part[chunk * 32 : (chunk + 1) * 32]
-        for chunk in range(4):
-            block = jnp.dot(gather, permuted[chunk], preferred_element_type=f32).astype(bf16)
-            results[group * 64 + chunk * 16 : group * 64 + (chunk + 1) * 16] = block.reshape(16, 16, 512)
-
-        def send_back(d, carry):
-            to = lax.rem(me + N_DEV * K_STEP - d * K_STEP, N_DEV)
+        for f in range(3):
+            width, start = WIDTHS[f] // 2, STARTS[f]
+            served = jnp.dot(active[...], down[:, start : start + 2 * width], preferred_element_type=f32).astype(bf16)
+            served = jnp.concatenate([served[:, :width], served[:, width:]], axis=0)
+            block = jnp.dot(gather[f], served, preferred_element_type=f32).astype(bf16)
+            results[f][group * 16 : (group + 1) * 16] = block.reshape(16, 16, width)
+
+            for j in range(group * 16 + first, group * 16 + 16):
+                pltpu.make_async_remote_copy(
+                    src_ref=results[f].at[j], dst_ref=returned[f].at[j], send_sem=back_sem.at[f],
+                    recv_sem=return_sem.at[f], device_id=across(f, j, -1), device_id_type=MESH,
+                ).start()
+            if group == 0:
+                returned[f][0] = results[f][0]
+
+    for f in range(3):
+        width, start = WIDTHS[f] // 2, STARTS[f]
+        landed = returned[f].at[pl.ds(1, 31)]
+        pltpu.make_async_copy(landed, landed, return_sem.at[f]).wait()
+        for h in range(2):
+            columns = slice(start + h * width, start + (h + 1) * width)
+            both = jnp.dot(mix[f, h], returned[f][...].reshape(512, width), preferred_element_type=f32)
+            both = both[:64] + both[64:]
+            state[:12, columns] = state[:12, columns] + both[:12]
+            for d in range(1, 4):
+                shared[f][d - 1, :, h * width : (h + 1) * width] = both[d * 16 : (d + 1) * 16].astype(bf16)
+        for d in (2, 1, 3):
             pltpu.make_async_remote_copy(
-                src_ref=results.at[d], dst_ref=returned.at[d], send_sem=back_sem.at[0],
-                recv_sem=return_sem.at[0], device_id=(to // 4, lax.rem(to, 4)), device_id_type=MESH,
+                src_ref=shared[f].at[d - 1], dst_ref=arrived[f].at[d - 1], send_sem=share_send_sem.at[f],
+                recv_sem=share_recv_sem.at[f], device_id=place(*ahead(f, 4 - d)), device_id_type=MESH,
             ).start()
-            return carry
-
-        lax.fori_loop(first, 64 * (group + 1), send_back, 0)
-        if group == 0:
-            returned[0] = results[0]
-
-    landed = returned.at[pl.ds(1, 127)]
-    pltpu.make_async_copy(landed, landed, return_sem.at[0]).wait()
-    both = jnp.dot(mix[...], returned[...].reshape(2048, 512), preferred_element_type=f32)
-    blended = both[:128] + both[128:]
-    for s in range(8):
-        columns = slice(s * 512, (s + 1) * 512)
-        total = state[:, columns] + blended[s * 16 : (s + 1) * 16]
-        out_ref[:, columns] = total[:12].astype(bf16)
-    gone = sent.at[pl.ds(1, 63)]
-    pltpu.make_async_copy(gone, gone, send_sem.at[0]).wait()
-    gone = sent.at[pl.ds(64, 64)]
-    pltpu.make_async_copy(gone, gone, send_sem.at[1]).wait()
-    gone = results.at[pl.ds(1, 127)]
-    pltpu.make_async_copy(gone, gone, back_sem.at[0]).wait()
+    for f in range(3):
+        columns = slice(STARTS[f], STARTS[f] + WIDTHS[f])
+        pltpu.make_async_copy(arrived[f], arrived[f], share_recv_sem.at[f]).wait()
+        total = state[:12, columns]
+        for d in range(3):
+            total = total + arrived[f][d, :12, :].astype(f32)
+        out_ref[:, columns] = total.astype(bf16)
+
     for n in range(6):
-        pltpu.make_async_copy(o_proj_hbm.at[pl.ds(0, 1024)], projection.at[pl.ds(0, 1024), pl.ds(128, 128)], o_send_sem.at[n]).wait()
+        pltpu.make_async_copy(
+            o_proj_hbm.at[pl.ds(0, 1024)], projection.at[pl.ds(0, 1024), pl.ds(128, 128)], o_send_sem.at[n]
+        ).wait()
     gone = gathered.at[pl.ds(1, 7)]
     pltpu.make_async_copy(gone, gone, a_send_sem).wait()
     gone = collected.at[pl.ds(1, 31)]
     pltpu.make_async_copy(gone, gone, p_send_sem).wait()
+    gone = tiles.at[pl.ds(0, 9)]
+    pltpu.make_async_copy(gone, gone, tile_send_sem).wait()
+    for f in range(3):
+        gone = line[f].at[pl.ds(1, 3)]
+        pltpu.make_async_copy(gone, gone, line_send_sem.at[f]).wait()
+        gone = sent[f].at[pl.ds(1, 31)]
+        pltpu.make_async_copy(gone, gone, send_sem.at[f]).wait()
+        gone = results[f].at[pl.ds(1, 31)]
+        pltpu.make_async_copy(gone, gone, back_sem.at[f]).wait()
+        pltpu.make_async_copy(shared[f], shared[f], share_send_sem.at[f]).wait()
 
 
 def body(
@@ -344,6 +420,7 @@
     vmem = pl.BlockSpec(memory_space=pltpu.VMEM)
     smem = pl.BlockSpec(memory_space=pltpu.SMEM)
     hbm = pl.BlockSpec(memory_space=pl.ANY)
+    each = lambda shape: tuple(shape(w) for w in WIDTHS)
     dma, plain = pltpu.SemaphoreType.DMA, pltpu.SemaphoreType.REGULAR
     return pl.pallas_call(
         kernel,
@@ -365,18 +442,23 @@
             pltpu.VMEM((16, 4096), f32),
             pltpu.VMEM((4096, 1536), bf16),
             pltpu.VMEM((768, 4096), bf16),
-            pltpu.VMEM((128, 16, 512), bf16),
-            pltpu.VMEM((128, 16, 512), bf16),
+            pltpu.VMEM((10, 16, 128), f32),
+            each(lambda w: pltpu.VMEM((4, 16, w), bf16)),
+            each(lambda w: pltpu.VMEM((32, 16, w // 2), bf16)),
+            each(lambda w: pltpu.VMEM((32, 16, w // 2), bf16)),
             pltpu.VMEM((128, 4096), bf16),
             pltpu.VMEM((128, 768), bf16),
-            pltpu.VMEM((4, 256, 512), bf16),
-            pltpu.VMEM((128, 16, 512), bf16),
-            pltpu.VMEM((128, 16, 512), bf16),
-            pltpu.VMEM((128, 512), bf16),
-            pltpu.VMEM((256, 2048), bf16),
-            pltpu.VMEM((2048, 128), bf16),
+            each(lambda w: pltpu.VMEM((32, 16, w // 2), bf16)),
+            each(lambda w: pltpu.VMEM((32, 16, w // 2), bf16)),
+            each(lambda w: pltpu.VMEM((3, 16, w), bf16)),
+            each(lambda w: pltpu.VMEM((3, 16, w), bf16)),
+            pltpu.VMEM((3, 256, 64), bf16),
+            pltpu.VMEM((3, 2, 128, 512), bf16),
+            pltpu.VMEM((3, 256, 256), bf16),
+            pltpu.VMEM((3, 256, 256), bf16),
             dma((2, 3)), dma((2,)), dma, dma((6,)), dma((6,)), dma, dma((3, 8)), dma, dma,
-            dma((2,)), dma((2,)), dma((1,)), dma((1,)), plain, plain,
+            dma, dma, dma((3,)), dma((3,)), dma((3,)), dma((3, 2)), dma((3,)), dma((3,)),
+            dma((3,)), dma((3,)), plain, plain,
         ],
         compiler_params=pltpu.CompilerParams(
             collective_id=1, has_side_effects=True, vmem_limit_bytes=60 * 2**20

time: 90.5 us -> 85.8 us (0.948)
  Pallas kernels: 88.8 us -> 83.9 us
    pallas_call x1, Pallas kernels: 88.8 us -> 83.9 us  [body(): pl.pallas_call(kernel, out_shape=jax.ShapeDtypeStruct((12, 4096), bf16),...]
where the time goes in v4:
time: 85.8 us; the launch traced here: 85.5 us
  Pallas kernels  83.9 us (98%)
  local copies, waits for them, and re-layouts  1.57 us (2%)
    pallas_call x1, Pallas kernels, body(): pl.pallas_call(kernel, out_shape=jax.ShapeDtypeStruct((12, 4096), bf16),...  83.9 us

profile of v4, /device:TPU:1, one launch (start us, length us, event | category | flops | bytes accessed | tf_op | source)
XLA Modules:
  0.0 85.5 jit_solution(1520623359540984574)
XLA Ops:
  0.0 83.9 %layer.1 = bf16[12,4096]{1,0:T(8,128)(2,1)} custom-call(bf16[48,2048]{1,0:T(8,128)(2,1)} %queries_ref.1, bf16[48,192,128]{2,1,0:T(8,128)(2,1)} %bitcast.9, bf16[48,192,128]{2,1,0:T(8,128)(2,1)} %bitcast.10, s32[48]{0:T(128)} %lengths_smem.1, bf16[2048,128]{1,0:T(8,128)(2,1)} %o_proj_hbm.1, bf16[12,4096]{1,0:T(8,128)(2,1)} %residual_ref.1, ...), custom_call_target="tpu_custom_call" | custom-call | flops 6000000000 | bytes 30000000 | tf_op jit(solution)/shard_map/layer/pallas_call | solution.py:425
  83.9 1.6 %copy.13 = bf16[12,4096]{1,0:T(8,128)(2,1)} copy(bf16[12,4096]{1,0:T(8,128)(2,1)} %layer.1) | data formatting | bytes 196608

commit v5 on v4

--- a/solution.py
+++ b/solution.py
@@ -26,8 +26,9 @@
     return lax.broadcasted_iota(jnp.int32, shape, dim)
 
 
-WIDTHS = (1536, 1280, 1280)
-STARTS = (0, 1536, 2816)
+WIDTHS = (1024, 1024, 1024)
+STARTS = (0, 1024, 2048)
+REST = 3072
 
 
 def ahead(axis, d):
@@ -36,14 +37,16 @@
 
 
 def kernel(
-    queries_ref, keys_hbm, values_hbm, lengths_smem, o_proj_hbm, residual_ref, gain_ref, routes_smem, weights_smem,
+    queries_hbm, keys_hbm, values_hbm, lengths_smem, o_proj_hbm, residual_hbm, gain_hbm, routes_smem, weights_smem,
     gate_up_hbm, down_hbm,
     out_ref,
-    keys, values, heads, attended, gathered, projection, partial, staged, pieces, collected, summed, state, gate_up,
-    down, tiles, line, sent, received, rows, active, results, returned, shared, arrived, table, mix, spread, gather,
-    cache_sem, weight_sem, o_own_sem, o_send_sem, o_recv_sem, a_send_sem, a_recv_sem, p_send_sem, p_recv_sem,
+    queries, residual, gain, keys, values, heads, attended, gathered, projection, partial, staged, pieces, collected, summed, state, gate_up,
+    down, tiles, line, sent, received, rows, active, results, returned, shared, arrived, table, mix, spread, gather, blend,
+    straight, straight_table, straight_mix, swap, out_straight, in_straight, back_straight, home_straight,
+    row_sem, cache_sem, weight_sem, o_own_sem, o_send_sem, o_recv_sem, a_send_sem, a_recv_sem, p_send_sem, p_recv_sem,
     tile_send_sem, tile_recv_sem, line_send_sem, line_recv_sem, send_sem, recv_sem, back_sem, return_sem,
-    share_send_sem, share_recv_sem, along_y, along_z,
+    share_send_sem, share_recv_sem, straight_send_sem, straight_recv_sem, straight_back_sem, straight_home_sem,
+    along_y, along_z,
 ):
     r, kv = lax.axis_index("req"), lax.axis_index("kvh")
     x, y, z, c = coords()
@@ -70,19 +73,18 @@
         part = pl.ds(m * 16, 16)
         return pltpu.make_async_copy(source.at[part], target.at[part], cache_sem.at[which, m])
 
-    for m in range(3):
-        cache_load(m, 0).start()
-        cache_load(m, 1).start()
+    small = [
+        pltpu.make_async_copy(source, target, row_sem.at[n])
+        for n, (source, target) in enumerate(((queries_hbm, queries), (residual_hbm, residual), (gain_hbm, gain)))
+    ]
+    small[0].start()
+    cache_load(0, 0).start()
+    cache_load(0, 1).start()
     o_own = pltpu.make_async_copy(o_proj_hbm, projection.at[:, pl.ds(0, 128)], o_own_sem)
-    o_own.start()
     loads = [
         pltpu.make_async_copy(gate_up_hbm, gate_up, weight_sem.at[0]),
         pltpu.make_async_copy(down_hbm, down, weight_sem.at[1]),
     ]
-    for load in loads:
-        load.start()
-    for h in range(16):
-        heads[:, h, :] = queries_ref[:, h * 128 : (h + 1) * 128].astype(f32)
 
     def o_copy(source, slot, part, n, dy, rows):
         return pltpu.make_async_remote_copy(
@@ -105,6 +107,13 @@
         o_first(n).start()
     for d in range(1, 4):
         pl.semaphore_signal(along_y, inc=1, device_id=place(x, y + d, z, c), device_id_type=MESH)
+
+    for m in range(1, 3):
+        cache_load(m, 0).start()
+        cache_load(m, 1).start()
+    small[0].wait()
+    for h in range(16):
+        heads[:, h, :] = queries[:, h * 128 : (h + 1) * 128].astype(f32)
 
     position = iota((192, 128), 0)
     request = iota((128, 128), 1) // 16
@@ -166,6 +175,12 @@
                 pl.semaphore_signal(along_z, inc=1, device_id=place(x, y, z + d, c), device_id_type=MESH)
             pl.semaphore_wait(along_z, 3)
         a_send(m)
+        if m == 0:
+            o_own.start()
+            small[1].start()
+            small[2].start()
+            for load in loads:
+                load.start()
     for n in range(2):
         pltpu.make_async_copy(o_proj_hbm.at[pl.ds(0, 1024)], projection.at[pl.ds(0, 1024), pl.ds(128, 128)], o_recv_sem.at[n]).wait()
         o_pass(n).start()
@@ -178,7 +193,9 @@
             a_copy(dz * 2, m, 0, 1).start()
 
     state[...] = jnp.zeros((16, 4096), f32)
-    state[:12, :] = residual_ref[...].astype(f32)
+    small[1].wait()
+    small[2].wait()
+    state[:12, :] = residual[...].astype(f32)
 
     lane = iota((8, 128), 1)
     sub = iota((8, 128), 0)
@@ -215,6 +232,37 @@
         i, j = iota((256, 256), 0), iota((256, 256), 1)
         spread[f] = jnp.where(j == column(i), 1.0, 0.0).astype(bf16)
         gather[f] = jnp.where(i == column(j), 1.0, 0.0).astype(bf16)
+
+    number = expert
+    ring, group = number // 4, number & 3
+    dx = ((ring & 1) * 2 + group // 2 + 4 - x) & 3
+    dy = (ring // 8 + 4 - y) & 3
+    dz = (((ring // 2) & 3) + 4 - z) & 3
+    dc = ((group & 1) + 2 - c) & 1
+    key = (dc * 64 + dx * 16 + dy * 4 + dz) * 2 + place_of
+    key = jnp.where(token < 12, key, -1)
+    for part in range(8):
+        row = iota((256, 128), 0) + part * 256
+        hit = jnp.zeros((256, 128), f32)
+        for k in range(8):
+            hit = jnp.where(row // 8 == key[k : k + 1, :], 1.0, hit)
+        hit = jnp.where((row & 7) == iota((256, 128), 1) // 16, hit, 0.0)
+        straight_table[part * 256 : (part + 1) * 256, :] = hit.astype(bf16)
+    key_column = jnp.transpose(key.astype(f32)).astype(jnp.int32)
+    gate_column = jnp.transpose(gates)
+    for part in range(8):
+        spot = iota((128, 256), 1) + part * 256
+        share = jnp.zeros((128, 256), f32)
+        for k in range(8):
+            share = jnp.where(spot // 8 == key_column[:, k : k + 1], gate_column[:, k : k + 1], share)
+        share = jnp.where((spot & 7) == iota((128, 256), 0) // 16, share, 0.0)
+        high = share.astype(bf16)
+        straight_mix[:128, part * 256 : (part + 1) * 256] = high
+        straight_mix[128:, part * 256 : (part + 1) * 256] = (share - high.astype(f32)).astype(bf16)
+    i, j = iota((256, 256), 0), iota((256, 256), 1)
+    swap[0] = jnp.where(j == (i & 31) * 8 + i // 32, 1.0, 0.0).astype(bf16)
+    swap[1] = jnp.where(i == (j & 31) * 8 + j // 32, 1.0, 0.0).astype(bf16)
+    straight[...] = jnp.zeros((128, 128), bf16)
 
     landed = tiles.at[pl.ds(0, 9)]
     pltpu.make_async_copy(landed, landed, tile_recv_sem).wait()
@@ -260,15 +308,14 @@
         for slot in range(1, 8):
             if not (slot == 1 and m == 0 or slot in (2, 4, 6) and m > 0):
                 a_wait(m, slot)
-    def hand_out(q, carry):
-        d, e = q // 4, lax.rem(q, 4)
-        to = lax.rem(kv + e, 4)
-        there = (y * 4 + lax.rem(z + d // 2, 4)) * 2 + lax.rem(half + lax.rem(d, 2), 2)
+    halves, lows = [half, 1 - half], [kv // 2, 1 - kv // 2]
+
+    def hand_out(d, e):
+        to = lows[e // 2] * 2 + cores[e % 2]
         pltpu.make_async_remote_copy(
-            src_ref=pieces.at[d * 4 + to], dst_ref=collected.at[q], send_sem=p_send_sem, recv_sem=p_recv_sem,
-            device_id=(there, to), device_id_type=MESH,
+            src_ref=pieces.at[d * 4 + to], dst_ref=collected.at[d * 4 + e], send_sem=p_send_sem, recv_sem=p_recv_sem,
+            device_id=((y * 4 + zs[d // 2]) * 2 + halves[d % 2], to), device_id_type=MESH,
         ).start()
-        return carry
 
     for turn in range(2):
         slots = slice(turn * 4, turn * 4 + 4)
@@ -283,7 +330,9 @@
                         slot * 48 + k * 12 : slot * 48 + (k + 1) * 12, w * 128 : (w + 1) * 128
                     ]
             pieces[d * 4 : d * 4 + 4] = staged[d * 4 : d * 4 + 4].astype(bf16)
-            lax.fori_loop(d * 4 + (d == 0), d * 4 + 4, hand_out, 0)
+            for e in range(4):
+                if d or e:
+                    hand_out(d, e)
     collected[0] = pieces[kv]
     landed = collected.at[pl.ds(1, 31)]
     pltpu.make_async_copy(landed, landed, p_recv_sem).wait()
@@ -302,12 +351,45 @@
     factor = lax.rsqrt(jnp.sum(square, axis=1, keepdims=True) * (1.0 / 4096.0) + 1e-06)
     for f in range(3):
         columns = slice(STARTS[f], STARTS[f] + WIDTHS[f])
-        line[f][0, :12, :] = (state[:12, columns] * factor * gain_ref[:, columns]).astype(bf16)
+        line[f][0, :12, :] = (state[:12, columns] * factor * gain[:, columns]).astype(bf16)
         for d in (2, 1, 3):
             pltpu.make_async_remote_copy(
                 src_ref=line[f].at[0], dst_ref=line[f].at[d], send_sem=line_send_sem.at[f],
                 recv_sem=line_recv_sem.at[f], device_id=place(*ahead(f, d)), device_id_type=MESH,
             ).start()
+
+    for s in range(8):
+        columns = slice(REST + s * 128, REST + (s + 1) * 128)
+        straight[s * 16 : s * 16 + 12, :] = (state[:12, columns] * factor * gain[:, columns]).astype(bf16)
+
+    def straight_sends(source, target, send_sems, recv_sems, group, sign):
+        def start(dx, dy, i, dz):
+            there = (lax.rem(y + dy, 4) * 4 + zs[sign * dz % 4]) * 2 + lax.rem(x + dx, 4) // 2
+            j = group * 64 + i * 4 + dz
+            pltpu.make_async_remote_copy(
+                src_ref=source.at[j], dst_ref=target.at[j], send_sem=send_sems.at[group], recv_sem=recv_sems.at[group],
+                device_id=(there, lax.rem(x + dx, 2) * 2 + cores[group]), device_id_type=MESH,
+            ).start()
+
+        def four(i, carry):
+            for dz in range(4):
+                start(sign * (i // 4) + 4, sign * lax.rem(i, 4) + 4, i, dz)
+            return carry
+
+        for dz in range(1 - group, 4):
+            start(0, 0, 0, dz)
+        lax.fori_loop(1, 16, four, 0)
+
+    def straight_out(group):
+        for part in range(group * 4, group * 4 + 4):
+            block = jnp.dot(
+                straight_table[part * 256 : (part + 1) * 256, :], straight[...], preferred_element_type=f32
+            ).astype(bf16)
+            out_straight[part * 16 : (part + 1) * 16] = block.reshape(16, 16, 128)
+        straight_sends(out_straight, in_straight, straight_send_sem, straight_recv_sem, group, 1)
+
+    straight_out(0)
+    in_straight[0] = out_straight[0]
 
     def across(f, j, sign):
         p, q, dc = sign * (j // 4 % 4), sign * (j % 4), j // 16
@@ -333,6 +415,7 @@
                         src_ref=sent[f].at[j], dst_ref=received[f].at[j], send_sem=send_sem.at[f],
                         recv_sem=recv_sem.at[f, group], device_id=across(f, j, 1), device_id_type=MESH,
                     ).start()
+    straight_out(1)
     for f in range(3):
         received[f][0] = sent[f][0]
 
@@ -346,6 +429,13 @@
             block = jnp.dot(spread[f], block, preferred_element_type=f32).astype(bf16)
             for h in range(2):
                 rows[:, start + h * width : start + (h + 1) * width] = block[h * 128 : (h + 1) * 128]
+        landed = in_straight.at[pl.ds(group * 64 + first, 64 - first)]
+        pltpu.make_async_copy(landed, landed, straight_recv_sem.at[group]).wait()
+        for chunk in range(4):
+            block = in_straight[group * 64 + chunk * 16 : group * 64 + (chunk + 1) * 16].reshape(256, 128)
+            block = jnp.dot(swap[0], block, preferred_element_type=f32).astype(bf16)
+            for s in range(8):
+                rows[chunk * 32 : (chunk + 1) * 32, REST + s * 128 : REST + (s + 1) * 128] = block[s * 32 : (s + 1) * 32]
         if group == 0:
             loads[0].wait()
         for n in range(3):
@@ -364,19 +454,40 @@
             for j in range(group * 16 + first, group * 16 + 16):
                 pltpu.make_async_remote_copy(
                     src_ref=results[f].at[j], dst_ref=returned[f].at[j], send_sem=back_sem.at[f],
-                    recv_sem=return_sem.at[f], device_id=across(f, j, -1), device_id_type=MESH,
+                    recv_sem=return_sem.at[f, group], device_id=across(f, j, -1), device_id_type=MESH,
                 ).start()
             if group == 0:
                 returned[f][0] = results[f][0]
 
+        served = jnp.dot(active[...], down[:, REST : REST + 1024], preferred_element_type=f32).astype(bf16)
+        for chunk in range(4):
+            block = jnp.concatenate(
+                [served[chunk * 32 : (chunk + 1) * 32, s * 128 : (s + 1) * 128] for s in range(8)], axis=0
+            )
+            block = jnp.dot(swap[1], block, preferred_element_type=f32).astype(bf16)
+            back_straight[group * 64 + chunk * 16 : group * 64 + (chunk + 1) * 16] = block.reshape(16, 16, 128)
+        straight_sends(back_straight, home_straight, straight_back_sem, straight_home_sem, group, -1)
+        if group == 0:
+            home_straight[0] = back_straight[0]
+
+    def mixed(f, group, h):
+        block = returned[f][group * 16 : (group + 1) * 16].reshape(256, WIDTHS[f] // 2)
+        both = jnp.dot(mix[f, h, :, group * 256 : (group + 1) * 256], block, preferred_element_type=f32)
+        return both[:64] + both[64:]
+
     for f in range(3):
         width, start = WIDTHS[f] // 2, STARTS[f]
-        landed = returned[f].at[pl.ds(1, 31)]
-        pltpu.make_async_copy(landed, landed, return_sem.at[f]).wait()
+        landed = returned[f].at[pl.ds(1, 15)]
+        pltpu.make_async_copy(landed, landed, return_sem.at[f, 0]).wait()
+        for h in range(2):
+            blend[:, start + h * width : start + (h + 1) * width] = mixed(f, 0, h)
+    for f in range(3):
+        width, start = WIDTHS[f] // 2, STARTS[f]
+        landed = returned[f].at[pl.ds(16, 16)]
+        pltpu.make_async_copy(landed, landed, return_sem.at[f, 1]).wait()
         for h in range(2):
             columns = slice(start + h * width, start + (h + 1) * width)
-            both = jnp.dot(mix[f, h], returned[f][...].reshape(512, width), preferred_element_type=f32)
-            both = both[:64] + both[64:]
+            both = blend[:, columns] + mixed(f, 1, h)
             state[:12, columns] = state[:12, columns] + both[:12]
             for d in range(1, 4):
                 shared[f][d - 1, :, h * width : (h + 1) * width] = both[d * 16 : (d + 1) * 16].astype(bf16)
@@ -385,6 +496,14 @@
                 src_ref=shared[f].at[d - 1], dst_ref=arrived[f].at[d - 1], send_sem=share_send_sem.at[f],
                 recv_sem=share_recv_sem.at[f], device_id=place(*ahead(f, 4 - d)), device_id_type=MESH,
             ).start()
+    for group in range(2):
+        landed = home_straight.at[pl.ds(group * 64 + 1 - group, 63 + group)]
+        pltpu.make_async_copy(landed, landed, straight_home_sem.at[group]).wait()
+    both = jnp.dot(straight_mix[...], home_straight[...].reshape(2048, 128), preferred_element_type=f32)
+    both = both[:128] + both[128:]
+    for s in range(8):
+        columns = slice(REST + s * 128, REST + (s + 1) * 128)
+        out_ref[:, columns] = (state[:12, columns] + both[s * 16 : s * 16 + 12]).astype(bf16)
     for f in range(3):
         columns = slice(STARTS[f], STARTS[f] + WIDTHS[f])
         pltpu.make_async_copy(arrived[f], arrived[f], share_recv_sem.at[f]).wait()
@@ -411,6 +530,11 @@
         gone = results[f].at[pl.ds(1, 31)]
         pltpu.make_async_copy(gone, gone, back_sem.at[f]).wait()
         pltpu.make_async_copy(shared[f], shared[f], share_send_sem.at[f]).wait()
+    for group in range(2):
+        gone = out_straight.at[pl.ds(group * 64 + 1 - group, 63 + group)]
+        pltpu.make_async_copy(gone, gone, straight_send_sem.at[group]).wait()
+        gone = back_straight.at[pl.ds(group * 64 + 1 - group, 63 + group)]
+        pltpu.make_async_copy(gone, gone, straight_back_sem.at[group]).wait()
 
 
 def body(
@@ -425,9 +549,12 @@
     return pl.pallas_call(
         kernel,
         out_shape=jax.ShapeDtypeStruct((12, 4096), bf16),
-        in_specs=[vmem, hbm, hbm, smem, hbm, vmem, vmem, smem, smem, hbm, hbm],
+        in_specs=[hbm, hbm, hbm, smem, hbm, hbm, hbm, smem, smem, hbm, hbm],
         out_specs=vmem,
         scratch_shapes=[
+            pltpu.VMEM((48, 2048), bf16),
+            pltpu.VMEM((12, 4096), bf16),
+            pltpu.VMEM((1, 4096), f32),
             pltpu.VMEM((48, 192, 128), bf16),
             pltpu.VMEM((48, 192, 128), bf16),
             pltpu.VMEM((48, 16, 128), f32),
@@ -456,9 +583,18 @@
             pltpu.VMEM((3, 2, 128, 512), bf16),
             pltpu.VMEM((3, 256, 256), bf16),
             pltpu.VMEM((3, 256, 256), bf16),
-            dma((2, 3)), dma((2,)), dma, dma((6,)), dma((6,)), dma, dma((3, 8)), dma, dma,
-            dma, dma, dma((3,)), dma((3,)), dma((3,)), dma((3, 2)), dma((3,)), dma((3,)),
-            dma((3,)), dma((3,)), plain, plain,
+            pltpu.VMEM((64, 3072), f32),
+            pltpu.VMEM((128, 128), bf16),
+            pltpu.VMEM((2048, 128), bf16),
+            pltpu.VMEM((256, 2048), bf16),
+            pltpu.VMEM((2, 256, 256), bf16),
+            pltpu.VMEM((128, 16, 128), bf16),
+            pltpu.VMEM((128, 16, 128), bf16),
+            pltpu.VMEM((128, 16, 128), bf16),
+            pltpu.VMEM((128, 16, 128), bf16),
+            dma((3,)), dma((2, 3)), dma((2,)), dma, dma((6,)), dma((6,)), dma, dma((3, 8)), dma, dma,
+            dma, dma, dma((3,)), dma((3,)), dma((3,)), dma((3, 2)), dma((3,)), dma((3, 2)),
+            dma((3,)), dma((3,)), dma((2,)), dma((2,)), dma((2,)), dma((2,)), plain, plain,
         ],
         compiler_params=pltpu.CompilerParams(
             collective_id=1, has_side_effects=True, vmem_limit_bytes=60 * 2**20

time: 85.8 us -> 83 us (0.967)
  Pallas kernels: 83.9 us -> 81.3 us
    pallas_call x1, Pallas kernels: 83.9 us -> 81.3 us  [body(): pl.pallas_call(kernel, out_shape=jax.ShapeDtypeStruct((12, 4096), bf16),...]
where the time goes in v5:
time: 83 us; the launch traced here: 82.8 us
  Pallas kernels  81.3 us (98%)
  local copies, waits for them, and re-layouts  1.57 us (2%)
    pallas_call x1, Pallas kernels, body(): pl.pallas_call(kernel, out_shape=jax.ShapeDtypeStruct((12, 4096), bf16),...  81.3 us

profile of v5, /device:TPU:1, one launch (start us, length us, event | category | flops | bytes accessed | tf_op | source)
XLA Modules:
  0.0 82.8 jit_solution(3852345969446206921)
XLA Ops:
  0.0 81.3 %layer.1 = bf16[12,4096]{1,0:T(8,128)(2,1)} custom-call(bf16[48,2048]{1,0:T(8,128)(2,1)} %queries_hbm.1, bf16[48,192,128]{2,1,0:T(8,128)(2,1)} %bitcast.9, bf16[48,192,128]{2,1,0:T(8,128)(2,1)} %bitcast.10, s32[48]{0:T(128)} %lengths_smem.1, bf16[2048,128]{1,0:T(8,128)(2,1)} %o_proj_hbm.1, bf16[12,4096]{1,0:T(8,128)(2,1)} %residual_hbm.1, ...), custom_call_target="tpu_custom_call" | custom-call | flops 6000000000 | bytes 30000000 | tf_op jit(solution)/shard_map/layer/pallas_call | solution.py:549
  81.3 1.6 %copy.13 = bf16[12,4096]{1,0:T(8,128)(2,1)} copy(bf16[12,4096]{1,0:T(8,128)(2,1)} %layer.1) | data formatting | bytes 196608

commit v6 on v5

--- a/solution.py
+++ b/solution.py
@@ -39,11 +39,11 @@
 def kernel(
     queries_hbm, keys_hbm, values_hbm, lengths_smem, o_proj_hbm, residual_hbm, gain_hbm, routes_smem, weights_smem,
     gate_up_hbm, down_hbm,
-    out_ref,
-    queries, residual, gain, keys, values, heads, attended, gathered, projection, partial, staged, pieces, collected, summed, state, gate_up,
+    out_hbm,
+    out_ref, queries, residual, gain, keys, values, heads, attended, gathered, projection, partial, staged, pieces, collected, summed, state, gate_up,
     down, tiles, line, sent, received, rows, active, results, returned, shared, arrived, table, mix, spread, gather, blend,
     straight, straight_table, straight_mix, swap, out_straight, in_straight, back_straight, home_straight,
-    row_sem, cache_sem, weight_sem, o_own_sem, o_send_sem, o_recv_sem, a_send_sem, a_recv_sem, p_send_sem, p_recv_sem,
+    out_sem, row_sem, cache_sem, weight_sem, o_own_sem, o_send_sem, o_recv_sem, a_send_sem, a_recv_sem, p_send_sem, p_recv_sem,
     tile_send_sem, tile_recv_sem, line_send_sem, line_recv_sem, send_sem, recv_sem, back_sem, return_sem,
     share_send_sem, share_recv_sem, straight_send_sem, straight_recv_sem, straight_back_sem, straight_home_sem,
     along_y, along_z,
@@ -60,13 +60,14 @@
         return ((ys[dy % 4] * 4 + zs[dz % 4]) * 2 + high_x[dx % 4], low_x[dx % 4] + cores[dc])
 
     barrier = pltpu.get_barrier_semaphore()
+    for d in range(1, 4):
+        pl.semaphore_signal(barrier, inc=1, device_id=away(0, d, 0, 0), device_id_type=MESH)
+    for d in range(1, 4):
+        pl.semaphore_signal(barrier, inc=1, device_id=away(0, 0, d, 0), device_id_type=MESH)
     for dx in range(4):
         for dc in range(2):
             if dx or dc:
-                pl.semaphore_signal(barrier, inc=1, device_id=place(x + dx, y, z, c + dc), device_id_type=MESH)
-    for d in range(1, 4):
-        pl.semaphore_signal(barrier, inc=1, device_id=place(x, y + d, z, c), device_id_type=MESH)
-        pl.semaphore_signal(barrier, inc=1, device_id=place(x, y, z + d, c), device_id_type=MESH)
+                pl.semaphore_signal(barrier, inc=1, device_id=away(dx, 0, 0, dc), device_id_type=MESH)
 
     def cache_load(m, which):
         source, target = ((keys_hbm, keys), (values_hbm, values))[which]
@@ -169,12 +170,13 @@
         attend(2 * m)
         attend(2 * m + 1)
         a_start(m)
-        if m == 0:
+        a_send(m)
+        if m == 1:
             pl.semaphore_wait(along_y, 3)
             for d in range(1, 4):
                 pl.semaphore_signal(along_z, inc=1, device_id=place(x, y, z + d, c), device_id_type=MESH)
+        if m == 2:
             pl.semaphore_wait(along_z, 3)
-        a_send(m)
         if m == 0:
             o_own.start()
             small[1].start()
@@ -409,7 +411,8 @@
             sent[f][group * 16 : (group + 1) * 16] = jnp.concatenate(
                 [block[:, :, :width], block[:, :, width:]], axis=1
             ).astype(bf16)
-            for j in blocks:
+        for j in blocks:
+            for f in range(3):
                 if j:
                     pltpu.make_async_remote_copy(
                         src_ref=sent[f].at[j], dst_ref=received[f].at[j], send_sem=send_sem.at[f],
@@ -451,14 +454,15 @@
             block = jnp.dot(gather[f], served, preferred_element_type=f32).astype(bf16)
             results[f][group * 16 : (group + 1) * 16] = block.reshape(16, 16, width)
 
-            for j in range(group * 16 + first, group * 16 + 16):
+            if group == 0:
+                returned[f][0] = results[f][0]
+
+        for j in range(group * 16 + first, group * 16 + 16):
+            for f in range(3):
                 pltpu.make_async_remote_copy(
                     src_ref=results[f].at[j], dst_ref=returned[f].at[j], send_sem=back_sem.at[f],
                     recv_sem=return_sem.at[f, group], device_id=across(f, j, -1), device_id_type=MESH,
                 ).start()
-            if group == 0:
-                returned[f][0] = results[f][0]
-
         served = jnp.dot(active[...], down[:, REST : REST + 1024], preferred_element_type=f32).astype(bf16)
         for chunk in range(4):
             block = jnp.concatenate(
@@ -504,6 +508,11 @@
     for s in range(8):
         columns = slice(REST + s * 128, REST + (s + 1) * 128)
         out_ref[:, columns] = (state[:12, columns] + both[s * 16 : s * 16 + 12]).astype(bf16)
+    def give(n, start, width):
+        part = pl.ds(start, width)
+        return pltpu.make_async_copy(out_ref.at[:, part], out_hbm.at[:, part], out_sem.at[n])
+
+    give(3, REST, 1024).start()
     for f in range(3):
         columns = slice(STARTS[f], STARTS[f] + WIDTHS[f])
         pltpu.make_async_copy(arrived[f], arrived[f], share_recv_sem.at[f]).wait()
@@ -511,6 +520,7 @@
         for d in range(3):
             total = total + arrived[f][d, :12, :].astype(f32)
         out_ref[:, columns] = total.astype(bf16)
+        give(f, STARTS[f], WIDTHS[f]).start()
 
     for n in range(6):
         pltpu.make_async_copy(
@@ -535,6 +545,9 @@
         pltpu.make_async_copy(gone, gone, straight_send_sem.at[group]).wait()
         gone = back_straight.at[pl.ds(group * 64 + 1 - group, 63 + group)]
         pltpu.make_async_copy(gone, gone, straight_back_sem.at[group]).wait()
+    for f in range(3):
+        give(f, STARTS[f], WIDTHS[f]).wait()
+    give(3, REST, 1024).wait()
 
 
 def body(
@@ -550,8 +563,9 @@
         kernel,
         out_shape=jax.ShapeDtypeStruct((12, 4096), bf16),
         in_specs=[hbm, hbm, hbm, smem, hbm, hbm, hbm, smem, smem, hbm, hbm],
-        out_specs=vmem,
+        out_specs=hbm,
         scratch_shapes=[
+            pltpu.VMEM((12, 4096), bf16),
             pltpu.VMEM((48, 2048), bf16),
             pltpu.VMEM((12, 4096), bf16),
             pltpu.VMEM((1, 4096), f32),
@@ -592,7 +606,7 @@
             pltpu.VMEM((128, 16, 128), bf16),
             pltpu.VMEM((128, 16, 128), bf16),
             pltpu.VMEM((128, 16, 128), bf16),
-            dma((3,)), dma((2, 3)), dma((2,)), dma, dma((6,)), dma((6,)), dma, dma((3, 8)), dma, dma,
+            dma((4,)), dma((3,)), dma((2, 3)), dma((2,)), dma, dma((6,)), dma((6,)), dma, dma((3, 8)), dma, dma,
             dma, dma, dma((3,)), dma((3,)), dma((3,)), dma((3, 2)), dma((3,)), dma((3, 2)),
             dma((3,)), dma((3,)), dma((2,)), dma((2,)), dma((2,)), dma((2,)), plain, plain,
         ],

time: 83 us -> 82.1 us (0.989)
  Pallas kernels: 81.3 us -> 80.3 us
    pallas_call x1, Pallas kernels: 81.3 us -> 80.3 us  [body(): pl.pallas_call(kernel, out_shape=jax.ShapeDtypeStruct((12, 4096), bf16),...]
where the time goes in v6:
time: 82.1 us; the launch traced here: 81.9 us
  Pallas kernels  80.3 us (98%)
  local copies, waits for them, and re-layouts  1.57 us (2%)
    pallas_call x1, Pallas kernels, body(): pl.pallas_call(kernel, out_shape=jax.ShapeDtypeStruct((12, 4096), bf16),...  80.3 us

profile of v6, /device:TPU:1, one launch (start us, length us, event | category | flops | bytes accessed | tf_op | source)
XLA Modules:
  0.0 81.9 jit_solution(14468622429330069153)
XLA Ops:
  0.0 80.3 %layer.1 = bf16[12,4096]{1,0:T(8,128)(2,1)} custom-call(bf16[48,2048]{1,0:T(8,128)(2,1)} %queries_hbm.1, bf16[48,192,128]{2,1,0:T(8,128)(2,1)} %bitcast.9, bf16[48,192,128]{2,1,0:T(8,128)(2,1)} %bitcast.10, s32[48]{0:T(128)} %lengths_smem.1, bf16[2048,128]{1,0:T(8,128)(2,1)} %o_proj_hbm.1, bf16[12,4096]{1,0:T(8,128)(2,1)} %residual_hbm.1, ...), custom_call_target="tpu_custom_call" | custom-call | flops 6000000000 | bytes 30000000 | tf_op jit(solution)/shard_map/layer/pallas_call | solution.py:562
  80.4 1.6 %copy.13 = bf16[12,4096]{1,0:T(8,128)(2,1)} copy(bf16[12,4096]{1,0:T(8,128)(2,1)} %layer.1) | data formatting | bytes 196608

commit v7 on v6

--- a/solution.py
+++ b/solution.py
@@ -224,17 +224,39 @@
             ).start()
         line[f][0] = jnp.zeros((16, WIDTHS[f]), bf16)
 
-    for f in range(3):
-        def column(i):
-            half_of, n = i // 128, i & 127
-            dx, dy, dz, row = n // 32, (n // 8) & 3, (n // 2) & 3, n & 1
-            p, q, g = ((dx, dy, dz), (dx, dz, dy), (dy, dz, dx))[f]
-            return (p * 4 + q) * 16 + half_of * 8 + g * 2 + row
-
-        i, j = iota((256, 256), 0), iota((256, 256), 1)
-        spread[f] = jnp.where(j == column(i), 1.0, 0.0).astype(bf16)
-        gather[f] = jnp.where(i == column(j), 1.0, 0.0).astype(bf16)
-
+    o_own.wait()
+    for n in range(2, 6):
+        pltpu.make_async_copy(o_proj_hbm.at[pl.ds(0, 1024)], projection.at[pl.ds(0, 1024), pl.ds(128, 128)], o_recv_sem.at[n]).wait()
+    for m in range(3):
+        for slot in range(1, 8):
+            if not (slot == 1 and m == 0 or slot in (2, 4, 6) and m > 0):
+                a_wait(m, slot)
+    halves, lows = [half, 1 - half], [kv // 2, 1 - kv // 2]
+
+    def hand_out(d, e):
+        to = lows[e // 2] * 2 + cores[e % 2]
+        pltpu.make_async_remote_copy(
+            src_ref=pieces.at[d * 4 + to], dst_ref=collected.at[d * 4 + e], send_sem=p_send_sem, recv_sem=p_recv_sem,
+            device_id=((y * 4 + zs[d // 2]) * 2 + halves[d % 2], to), device_id_type=MESH,
+        ).start()
+
+    for turn in range(2):
+        slots = slice(turn * 4, turn * 4 + 4)
+        partial[turn * 192 : (turn + 1) * 192, :] = jnp.dot(
+            gathered[slots].reshape(192, 2048), projection[...], preferred_element_type=f32
+        )
+        for slot in range(turn * 4, turn * 4 + 4):
+            d = ((4 - slot // 2) % 4) * 2 + slot % 2
+            for k in range(4):
+                for w in range(4):
+                    staged[d * 4 + k, w * 12 : (w + 1) * 12, :] = partial[
+                        slot * 48 + k * 12 : slot * 48 + (k + 1) * 12, w * 128 : (w + 1) * 128
+                    ]
+            pieces[d * 4 : d * 4 + 4] = staged[d * 4 : d * 4 + 4].astype(bf16)
+            for e in range(4):
+                if d or e:
+                    hand_out(d, e)
+    collected[0] = pieces[kv]
     number = expert
     ring, group = number // 4, number & 3
     dx = ((ring & 1) * 2 + group // 2 + 4 - x) & 3
@@ -250,24 +272,12 @@
             hit = jnp.where(row // 8 == key[k : k + 1, :], 1.0, hit)
         hit = jnp.where((row & 7) == iota((256, 128), 1) // 16, hit, 0.0)
         straight_table[part * 256 : (part + 1) * 256, :] = hit.astype(bf16)
-    key_column = jnp.transpose(key.astype(f32)).astype(jnp.int32)
-    gate_column = jnp.transpose(gates)
-    for part in range(8):
-        spot = iota((128, 256), 1) + part * 256
-        share = jnp.zeros((128, 256), f32)
-        for k in range(8):
-            share = jnp.where(spot // 8 == key_column[:, k : k + 1], gate_column[:, k : k + 1], share)
-        share = jnp.where((spot & 7) == iota((128, 256), 0) // 16, share, 0.0)
-        high = share.astype(bf16)
-        straight_mix[:128, part * 256 : (part + 1) * 256] = high
-        straight_mix[128:, part * 256 : (part + 1) * 256] = (share - high.astype(f32)).astype(bf16)
-    i, j = iota((256, 256), 0), iota((256, 256), 1)
-    swap[0] = jnp.where(j == (i & 31) * 8 + i // 32, 1.0, 0.0).astype(bf16)
-    swap[1] = jnp.where(i == (j & 31) * 8 + j // 32, 1.0, 0.0).astype(bf16)
+    own_key, own_gates = key, gates
     straight[...] = jnp.zeros((128, 128), bf16)
 
     landed = tiles.at[pl.ds(0, 9)]
     pltpu.make_async_copy(landed, landed, tile_recv_sem).wait()
+    line_tables = []
     for f in range(3):
         marks = jnp.full((8, 128), -1, jnp.int32)
         gates = jnp.zeros((8, 128), f32)
@@ -289,53 +299,8 @@
         for k in range(8):
             hit = jnp.where(row == key[k : k + 1, :64], 1.0, hit)
         table[f] = hit.astype(bf16)
-        key_column = jnp.transpose(key.astype(f32))[:64].astype(jnp.int32)
-        gate_column = jnp.transpose(gates)[:64]
-        spot = iota((64, 512), 1)
-        share = jnp.zeros((64, 512), f32)
-        for k in range(8):
-            share = jnp.where(
-                (spot // 16) * 8 + (spot & 7) == key_column[:, k : k + 1], gate_column[:, k : k + 1], share
-            )
-        for h in range(2):
-            part = jnp.where((spot // 8) & 1 == h, share, 0.0)
-            high = part.astype(bf16)
-            mix[f, h, :64, :] = high
-            mix[f, h, 64:, :] = (part - high.astype(f32)).astype(bf16)
-
-    o_own.wait()
-    for n in range(2, 6):
-        pltpu.make_async_copy(o_proj_hbm.at[pl.ds(0, 1024)], projection.at[pl.ds(0, 1024), pl.ds(128, 128)], o_recv_sem.at[n]).wait()
-    for m in range(3):
-        for slot in range(1, 8):
-            if not (slot == 1 and m == 0 or slot in (2, 4, 6) and m > 0):
-                a_wait(m, slot)
-    halves, lows = [half, 1 - half], [kv // 2, 1 - kv // 2]
-
-    def hand_out(d, e):
-        to = lows[e // 2] * 2 + cores[e % 2]
-        pltpu.make_async_remote_copy(
-            src_ref=pieces.at[d * 4 + to], dst_ref=collected.at[d * 4 + e], send_sem=p_send_sem, recv_sem=p_recv_sem,
-            device_id=((y * 4 + zs[d // 2]) * 2 + halves[d % 2], to), device_id_type=MESH,
-        ).start()
-
-    for turn in range(2):
-        slots = slice(turn * 4, turn * 4 + 4)
-        partial[turn * 192 : (turn + 1) * 192, :] = jnp.dot(
-            gathered[slots].reshape(192, 2048), projection[...], preferred_element_type=f32
-        )
-        for slot in range(turn * 4, turn * 4 + 4):
-            d = ((4 - slot // 2) % 4) * 2 + slot % 2
-            for k in range(4):
-                for w in range(4):
-                    staged[d * 4 + k, w * 12 : (w + 1) * 12, :] = partial[
-                        slot * 48 + k * 12 : slot * 48 + (k + 1) * 12, w * 128 : (w + 1) * 128
-                    ]
-            pieces[d * 4 : d * 4 + 4] = staged[d * 4 : d * 4 + 4].astype(bf16)
-            for e in range(4):
-                if d or e:
-                    hand_out(d, e)
-    collected[0] = pieces[kv]
+        line_tables.append((key, gates))
+
     landed = collected.at[pl.ds(1, 31)]
     pltpu.make_async_copy(landed, landed, p_recv_sem).wait()
     square = jnp.zeros((12, 128), f32)
@@ -421,6 +386,46 @@
     straight_out(1)
     for f in range(3):
         received[f][0] = sent[f][0]
+
+    for f in range(3):
+        def column(i):
+            half_of, n = i // 128, i & 127
+            dx, dy, dz, row = n // 32, (n // 8) & 3, (n // 2) & 3, n & 1
+            p, q, g = ((dx, dy, dz), (dx, dz, dy), (dy, dz, dx))[f]
+            return (p * 4 + q) * 16 + half_of * 8 + g * 2 + row
+
+        i, j = iota((256, 256), 0), iota((256, 256), 1)
+        spread[f] = jnp.where(j == column(i), 1.0, 0.0).astype(bf16)
+        gather[f] = jnp.where(i == column(j), 1.0, 0.0).astype(bf16)
+
+    i, j = iota((256, 256), 0), iota((256, 256), 1)
+    swap[0] = jnp.where(j == (i & 31) * 8 + i // 32, 1.0, 0.0).astype(bf16)
+    swap[1] = jnp.where(i == (j & 31) * 8 + j // 32, 1.0, 0.0).astype(bf16)
+    key_column = jnp.transpose(own_key.astype(f32)).astype(jnp.int32)
+    gate_column = jnp.transpose(own_gates)
+    for part in range(8):
+        spot = iota((128, 256), 1) + part * 256
+        share = jnp.zeros((128, 256), f32)
+        for k in range(8):
+            share = jnp.where(spot // 8 == key_column[:, k : k + 1], gate_column[:, k : k + 1], share)
+        share = jnp.where((spot & 7) == iota((128, 256), 0) // 16, share, 0.0)
+        high = share.astype(bf16)
+        straight_mix[:128, part * 256 : (part + 1) * 256] = high
+        straight_mix[128:, part * 256 : (part + 1) * 256] = (share - high.astype(f32)).astype(bf16)
+    for f, (key, gates) in enumerate(line_tables):
+        key_column = jnp.transpose(key.astype(f32))[:64].astype(jnp.int32)
+        gate_column = jnp.transpose(gates)[:64]
+        spot = iota((64, 512), 1)
+        share = jnp.zeros((64, 512), f32)
+        for k in range(8):
+            share = jnp.where(
+                (spot // 16) * 8 + (spot & 7) == key_column[:, k : k + 1], gate_column[:, k : k + 1], share
+            )
+        for h in range(2):
+            part = jnp.where((spot // 8) & 1 == h, share, 0.0)
+            high = part.astype(bf16)
+            mix[f, h, :64, :] = high
+            mix[f, h, 64:, :] = (part - high.astype(f32)).astype(bf16)
 
     for group in range(2):
         first = 1 - group

time: 82.1 us -> 80.5 us (0.981)
  Pallas kernels: 80.3 us -> 78.8 us
    pallas_call x1, Pallas kernels: 80.3 us -> 78.8 us  [body(): pl.pallas_call(kernel, out_shape=jax.ShapeDtypeStruct((12, 4096), bf16),...]
where the time goes in v7:
time: 80.5 us; the launch traced here: 80.4 us
  Pallas kernels  78.8 us (98%)
  local copies, waits for them, and re-layouts  1.57 us (2%)
    pallas_call x1, Pallas kernels, body(): pl.pallas_call(kernel, out_shape=jax.ShapeDtypeStruct((12, 4096), bf16),...  78.8 us

profile of v7, /device:TPU:1, one launch (start us, length us, event | category | flops | bytes accessed | tf_op | source)
XLA Modules:
  0.0 80.4 jit_solution(2845249489211561850)
XLA Ops:
  0.0 78.8 %layer.1 = bf16[12,4096]{1,0:T(8,128)(2,1)} custom-call(bf16[48,2048]{1,0:T(8,128)(2,1)} %queries_hbm.1, bf16[48,192,128]{2,1,0:T(8,128)(2,1)} %bitcast.9, bf16[48,192,128]{2,1,0:T(8,128)(2,1)} %bitcast.10, s32[48]{0:T(128)} %lengths_smem.1, bf16[2048,128]{1,0:T(8,128)(2,1)} %o_proj_hbm.1, bf16[12,4096]{1,0:T(8,128)(2,1)} %residual_hbm.1, ...), custom_call_target="tpu_custom_call" | custom-call | flops 6000000000 | bytes 30000000 | tf_op jit(solution)/shard_map/layer/pallas_call | solution.py:567
  78.8 1.6 %copy.13 = bf16[12,4096]{1,0:T(8,128)(2,1)} copy(bf16[12,4096]{1,0:T(8,128)(2,1)} %layer.1) | data formatting | bytes 196608

commit v8 on v7

--- a/solution.py
+++ b/solution.py
@@ -225,12 +225,15 @@
         line[f][0] = jnp.zeros((16, WIDTHS[f]), bf16)
 
     o_own.wait()
-    for n in range(2, 6):
+    for n in range(2, 4):
         pltpu.make_async_copy(o_proj_hbm.at[pl.ds(0, 1024)], projection.at[pl.ds(0, 1024), pl.ds(128, 128)], o_recv_sem.at[n]).wait()
     for m in range(3):
         for slot in range(1, 8):
             if not (slot == 1 and m == 0 or slot in (2, 4, 6) and m > 0):
                 a_wait(m, slot)
+    partial[:, :256] = jnp.dot(gathered[...].reshape(384, 2048), projection[:, :256], preferred_element_type=f32)
+    for n in range(4, 6):
+        pltpu.make_async_copy(o_proj_hbm.at[pl.ds(0, 1024)], projection.at[pl.ds(0, 1024), pl.ds(128, 128)], o_recv_sem.at[n]).wait()
     halves, lows = [half, 1 - half], [kv // 2, 1 - kv // 2]
 
     def hand_out(d, e):
@@ -242,8 +245,8 @@
 
     for turn in range(2):
         slots = slice(turn * 4, turn * 4 + 4)
-        partial[turn * 192 : (turn + 1) * 192, :] = jnp.dot(
-            gathered[slots].reshape(192, 2048), projection[...], preferred_element_type=f32
+        partial[turn * 192 : (turn + 1) * 192, 256:] = jnp.dot(
+            gathered[slots].reshape(192, 2048), projection[:, 256:], preferred_element_type=f32
         )
         for slot in range(turn * 4, turn * 4 + 4):
             d = ((4 - slot // 2) % 4) * 2 + slot % 2

time: 80.5 us -> 80.6 us (level)
  no operation moved by 1% of the time
where the time goes in v8:
time: 80.6 us; the launch traced here: 80.4 us
  Pallas kernels  78.9 us (98%)
  local copies, waits for them, and re-layouts  1.57 us (2%)
    pallas_call x1, Pallas kernels, body(): pl.pallas_call(kernel, out_shape=jax.ShapeDtypeStruct((12, 4096), bf16),...  78.9 us

profile of v8, /device:TPU:1, one launch (start us, length us, event | category | flops | bytes accessed | tf_op | source)
XLA Modules:
  0.0 80.4 jit_solution(18227760250279657883)
XLA Ops:
  0.0 78.9 %layer.1 = bf16[12,4096]{1,0:T(8,128)(2,1)} custom-call(bf16[48,2048]{1,0:T(8,128)(2,1)} %queries_hbm.1, bf16[48,192,128]{2,1,0:T(8,128)(2,1)} %bitcast.9, bf16[48,192,128]{2,1,0:T(8,128)(2,1)} %bitcast.10, s32[48]{0:T(128)} %lengths_smem.1, bf16[2048,128]{1,0:T(8,128)(2,1)} %o_proj_hbm.1, bf16[12,4096]{1,0:T(8,128)(2,1)} %residual_hbm.1, ...), custom_call_target="tpu_custom_call" | custom-call | flops 6000000000 | bytes 30000000 | tf_op jit(solution)/shard_map/layer/pallas_call | solution.py:570
  78.9 1.6 %copy.13 = bf16[12,4096]{1,0:T(8,128)(2,1)} copy(bf16[12,4096]{1,0:T(8,128)(2,1)} %layer.1) | data formatting | bytes 196608
